TPU v7x, 256 devices: a whole 4x4x8 slice. The times are simulated.
256 devices in a mesh: frames: 64 (over y_hi, z, x), heads: 4 (over y_lo, core).
Axes of the slice: x: 4, y: 4 (y_hi: 2, y_lo: 2; y = y_hi * 2 + y_lo), z: 8, core: 2. Of those that a mesh axis runs over, the one named last changes fastest.
Arguments:
- frame_q: bfloat16 [256, 256, 5120], P('frames', None, 'heads'), may hold values from -200 to 200
- frame_k: bfloat16 [256, 256, 5120], P('frames', None, 'heads'), may hold values from -8 to 8
- frame_v: bfloat16 [256, 256, 5120], P('frames', None, 'heads'), may hold values from -6 to 6
- keyframe_q: bfloat16 [2048, 5120], P(('frames', 'heads')), may hold values from -200 to 200
- keyframe_k: bfloat16 [2048, 5120], P(('frames', 'heads')), may hold values from -8 to 8
- keyframe_v: bfloat16 [2048, 5120], P(('frames', 'heads')), may hold values from -6 to 6
- neighbours: int32 [64, 2], P('frames'), may hold values from 0 to 7
Outputs:
- frame_out: bfloat16 [256, 256, 5120], P('frames', None, 'heads')
- keyframe_out: bfloat16 [2048, 5120], P('frames', 'heads')
All inputs are finite; a program needn't handle non-finite values.
Results may differ from a plain program's by a relative error of at most 0.0047.
Values may be sent and summed in bfloat16 or wider, within the bound.
A program may use at most 128 MiB of HBM per device.

v0:
```python
import math

import jax
import jax.numpy as jnp
from jax import lax
from jax.sharding import PartitionSpec as P

HEAD_FEATURES = 128


def passed_along(array, axis, by):
    devices = lax.axis_size(axis)
    pairs = [(i, i + by) for i in range(devices) if 0 <= i + by < devices]
    return lax.ppermute(array, axis, pairs)


def attend(queries, keys_set, values_set, usable):
    row_count = queries.shape[0]
    key_count = keys_set.shape[0]
    head_count = queries.shape[1] // HEAD_FEATURES
    query_head_rows = queries.reshape(row_count, head_count, HEAD_FEATURES)
    key_head_rows = keys_set.reshape(key_count, head_count, HEAD_FEATURES)
    value_head_rows = values_set.reshape(key_count, head_count, HEAD_FEATURES)
    score_matrix = jnp.einsum(
        "gia,xia->igx", query_head_rows, key_head_rows, preferred_element_type=jnp.float32
    ) / math.sqrt(HEAD_FEATURES)
    score_matrix = jnp.where(usable[None, None, :], score_matrix, -jnp.inf)
    highest = jnp.max(score_matrix, axis=-1, keepdims=True)
    weights = jnp.exp(score_matrix - highest)
    totals = jnp.sum(weights, axis=-1)
    blended_output = jnp.einsum(
        "wqt,twx->qwx",
        weights.astype(jnp.bfloat16),
        value_head_rows,
        preferred_element_type=jnp.float32,
    )
    result = blended_output / jnp.transpose(totals)[:, :, None]
    return result.reshape(row_count, head_count * HEAD_FEATURES).astype(jnp.bfloat16)


def local(frame_q, frame_k, frame_v, keyframe_q, keyframe_k, keyframe_v, neighbours):
    frame_count = frame_q.shape[0]
    token_count = frame_q.shape[1]
    feature_width = frame_q.shape[2]
    position = lax.axis_index("frames")
    group_size = lax.axis_size("frames")
    local_q, local_k, local_v = (
        lax.all_to_all(keyframe_q, "heads", split_axis=1, concat_axis=0, tiled=True),
        lax.all_to_all(keyframe_k, "heads", split_axis=1, concat_axis=0, tiled=True),
        lax.all_to_all(keyframe_v, "heads", split_axis=1, concat_axis=0, tiled=True),
    )
    edge_first = jnp.concatenate([frame_k[0], frame_v[0]], axis=1)
    edge_last = jnp.concatenate([frame_k[-1], frame_v[-1]], axis=1)
    before = passed_along(edge_last, "frames", 1)
    after = passed_along(edge_first, "frames", -1)
    left_id = neighbours[0, 0]
    right_id = neighbours[0, 1]
    all_k, all_v = (
        lax.all_gather(local_k, "frames", axis=0, tiled=True),
        lax.all_gather(local_v, "frames", axis=0, tiled=True),
    )
    keyframe_out = attend(local_q, all_k, all_v, jnp.ones((all_k.shape[0],), jnp.bool_))
    picked_k = jnp.concatenate(
        [
            lax.dynamic_slice_in_dim(all_k, left_id * token_count, token_count, 0),
            lax.dynamic_slice_in_dim(all_k, right_id * token_count, token_count, 0),
        ],
        axis=0,
    )
    picked_v = jnp.concatenate(
        [
            lax.dynamic_slice_in_dim(all_v, left_id * token_count, token_count, 0),
            lax.dynamic_slice_in_dim(all_v, right_id * token_count, token_count, 0),
        ],
        axis=0,
    )
    stacked_k = jnp.concatenate(
        [before[None, :, :feature_width], frame_k, after[None, :, :feature_width]], axis=0
    )
    stacked_v = jnp.concatenate(
        [before[None, :, feature_width:], frame_v, after[None, :, feature_width:]], axis=0
    )

    def one_frame(frame_index):
        window_k = lax.dynamic_slice_in_dim(stacked_k, frame_index, 3, 0).reshape(
            3 * token_count, feature_width
        )
        window_v = lax.dynamic_slice_in_dim(stacked_v, frame_index, 3, 0).reshape(
            3 * token_count, feature_width
        )
        keys_set = jnp.concatenate([window_k, picked_k], axis=0)
        values_set = jnp.concatenate([window_v, picked_v], axis=0)
        first_ok = (frame_index > 0) | (position > 0)
        last_ok = (frame_index < frame_count - 1) | (position < group_size - 1)
        usable = jnp.concatenate(
            [
                jnp.full((token_count,), first_ok),
                jnp.ones((token_count,), jnp.bool_),
                jnp.full((token_count,), last_ok),
                jnp.ones((2 * token_count,), jnp.bool_),
            ]
        )
        return attend(frame_q[frame_index], keys_set, values_set, usable)

    frame_out = lax.map(one_frame, jnp.arange(frame_count, dtype=jnp.int32))
    return (frame_out, keyframe_out)


def solution(mesh):
    placed = (
        P("frames", None, "heads"),
        P("frames", None, "heads"),
        P("frames", None, "heads"),
        P(("frames", "heads"), None),
        P(("frames", "heads"), None),
        P(("frames", "heads"), None),
        P("frames", None),
    )
    return jax.shard_map(
        local,
        mesh=mesh,
        in_specs=placed,
        out_specs=(P("frames", None, "heads"), P("frames", "heads")),
        check_vma=False,
    )
```

profile of v0, /device:TPU:8, one launch (start us, length us, event | category | flops | bytes accessed | tf_op | source)
XLA Modules:
  0.0 531.5 jit_solution(5252393917560954623)
XLA Ops:
  7.2 8.6 %all_to_all.54 = bf16[8,4,1280]{2,0,1:T(8,128)(2,1)} all-to-all(bf16[8,4,1280]{2,0,1:T(8,128)(2,1)} %bitcast.93), channel_id=1, replica_groups=mesh['frames'=64,'heads'=4] {'heads'}, dimensions={1} | all-to-all | bytes 163840 | tf_op jit(solution)/shard_map/all_to_all | solution.py:49
  15.9 8.2 %all_to_all.55 = bf16[8,4,1280]{2,0,1:T(8,128)(2,1)} all-to-all(bf16[8,4,1280]{2,0,1:T(8,128)(2,1)} %bitcast.94), channel_id=1, replica_groups=mesh['frames'=64,'heads'=4] {'heads'}, dimensions={1} | all-to-all | bytes 163840 | tf_op jit(solution)/shard_map/all_to_all | solution.py:50
  29.7 5.6 %collective-permute-start = (bf16[256,2560]{1,0:T(8,128)(2,1)}, bf16[256,2560]{1,0:T(8,128)(2,1)}, u32[]{:S(2)}, u32[]{:S(2)}) collective-permute-start(bf16[256,2560]{1,0:T(8,128)(2,1)} %pad_maximum_fusion.2), channel_id=1, source_target_pairs={{0,4},{4,8},{8,12},{12,16},{16,20},{20,24},{24,28},{28,32},{32,36}... | collective-permute-start | bytes 3932168 | tf_op jit(solution)/shard_map/ppermute | solution.py:14
  35.3 5.0 all-to-all-start.2
  45.6 4.0 copy.41
  49.7 11.2 %collective-permute-done.1 = bf16[256,2560]{1,0:T(8,128)(2,1)} collective-permute-done((bf16[256,2560]{1,0:T(8,128)(2,1)}, bf16[256,2560]{1,0:T(8,128)(2,1)}, u32[]{:S(2)}, u32[]{:S(2)}) %collective-permute-start.1) | collective-permute-done | bytes 1310752 | tf_op jit(solution)/shard_map/ppermute | solution.py:14
  77.5 7.7 %pad_maximum_fusion.1 = bf16[6,256,1280]{1,0,2:T(8,128)(2,1)} fusion(bf16[1,256,1280]{1,0,2:T(2,128)(2,1)} %copy.45, bf16[4,256,1280]{1,0,2:T(4,128)(2,1)} %copy.44, bf16[1,256,1280]{1,0,2:T(2,128)(2,1)} %copy.43), kind=kLoop, calls=%fused_computation.30 | loop fusion | flops 11796480 | bytes 7864320 | tf_op jit(solution)/shard_map/concatenate | solution.py:77
  85.2 5.7 %pad_maximum_fusion = bf16[6,256,1280]{1,0,2:T(8,128)(2,1)} fusion(bf16[1,256,1280]{1,0,2:T(2,128)(2,1)S(1)} %copy-done.4, bf16[4,256,1280]{1,0,2:T(4,128)(2,1)S(1)} %copy.41, bf16[1,256,1280]{1,0,2:T(2,128)(2,1)S(1)} %copy-done.5), kind=kLoop, calls=%fused_computation.29 | loop fusion | flops 11796480 | bytes 7864320 | tf_op jit(solution)/shard_map/concatenate | solution.py:80
  90.9 59.5 %all-gather.5.cloned.1.call-done = bf16[2048,1280]{1,0:T(8,128)(2,1)} async-done(((bf16[32,1280]{1,0:T(8,128)(2,1)}), bf16[2048,1280]{1,0:T(8,128)(2,1)}) %all-gather.5.cloned.1.call-update) | async-done | bytes 5242896 | tf_op jit(solution)/shard_map/all_gather | solution.py:59
  150.4 132.2 %all-gather.3.cloned.1.call-done = bf16[2048,1280]{1,0:T(8,128)(2,1)} async-done(((bf16[32,1280]{1,0:T(8,128)(2,1)}), bf16[2048,1280]{1,0:T(8,128)(2,1)}) %all-gather.3.cloned.1.call-update) | async-done | bytes 5242896 | tf_op jit(solution)/shard_map/all_gather | solution.py:60
  285.8 8.0 %copy.51 = bf16[2048,1280]{0,1:T(8,128)(2,1)} copy(bf16[2048,1280]{1,0:T(8,128)(2,1)} %all-gather.5.cloned.1.call-done) | data formatting | bytes 10485760 | tf_op jit(solution)/shard_map/all_gather | solution.py:59
  297.7 7.9 %copy.54 = bf16[2048,1280]{0,1:T(8,128)(2,1)} copy(bf16[2048,1280]{1,0:T(8,128)(2,1)} %all-gather.3.cloned.1.call-done) | data formatting | bytes 10485760 | tf_op jit(solution)/shard_map/all_gather | solution.py:60
  305.6 4.4 fusion.44
  316.4 208.3 %while.12 = (s32[]{:T(128)}, bf16[4,256,1280]{2,1,0:T(8,128)(2,1)}, s32[4]{0:T(128)S(1)}, bf16[6,256,1280]{1,0,2:T(8,128)(2,1)}, bf16[256,1280]{0,1:T(8,128)(2,1...) while((s32[]{:T(128)}, bf16[4,256,1280]{2,1,0:T(8,128)(2,1)}, ...), condition=%wide.region_3.4_spmd, body=%wide.region_0.3_spmd.sunk | while | flops 1734081280 | bytes 132441968 | solution.py:105
  326.1 7.4 %constant_dynamic-slice_fusion.10 = (bf16[3,256,1280]{1,0,2:T(4,128)(2,1)}, bf16[3,256,1280]{1,0,2:T(4,128)(2,1)S(1)}) fusion(bf16[6,256,1280]{1,0,2:T(8,128)(2,1)} %get-tuple-element.339, s32[]{:T(128)S(6)} %select_n.52, bf16[6,256,1280]{1,0,2:T(8,128)(2,1)} %get-tuple-element.333), kind=kLoop, calls=%fused_computation.22.clone.1 | loop fusion | bytes 7864324 | tf_op jit(solution)/shard_map/while/body/eval_jaxpr/dynamic_slice | solution.py:85
  333.5 6.4 %concatenate.47 = bf16[768,10,128]{0,2,1:T(8,128)(2,1)} reshape(bf16[3,256,1280]{1,0,2:T(4,128)(2,1)} %get-tuple-element.290) | data formatting | bytes 3932160 | tf_op jit(solution)/shard_map/while/body/eval_jaxpr/concatenate | solution.py:91
  339.9 4.0 copy.79
  347.5 6.3 %fusion.61 = (f32[10,256]{1,0:T(8,128)S(1)}, f32[10,256,1280]{2,1,0:T(8,128)S(1)}) fusion(pred[1280]{0:T(1024)(128)(4,1)S(1)} %pad_add_fusion.2, bf16[256,10,128]{0,2,1:T(8,128)(2,1)} %bitcast.87, bf16[256,10,128]{2,0,1:T(8,128)(2,1)} %copy.77, bf16[256,10,128]{2,0,1:T(8,128)(2,1)} %copy.78, bf16[768,10,128]{2,0,1:T(8,128)(2,1)} %copy.79), kind=kOutput, calls=%fused_computation.2.clone.1 | convolution fusion | flops 858519040 | bytes 17050880 | tf_op jit(solution)/shard_map/while/body/eval_jaxpr/gia,xia->igx/dot_general | solution.py:24
  358.5 8.8 %divide_convert_fusion.2 = bf16[256,10,128]{0,2,1:T(8,128)(2,1)S(1)} fusion(f32[10,256,1280]{2,1,0:T(8,128)} %copy-done, f32[10,256]{1,0:T(8,128)S(1)} %get-tuple-element.292, pred[1280]{0:T(1024)(128)(4,1)S(1)} %pad_add_fusion.2, bf16[256,10,128]{0,2,1:T(8,128)(2,1)} %bitcast.79, bf16[256,10,128]{0,2,1:T(8,128)(2,1)} %bitcast.80, ...), kind=kOutput, calls=%fused_computation.19.clone.1 | convolution fusion | flops 862453760 | bytes 17061120 | tf_op jit(solution)/shard_map/while/body/eval_jaxpr/wqt,twx->qwx/dot_general | solution.py:31
  378.1 7.4 %constant_dynamic-slice_fusion.10 = (bf16[3,256,1280]{1,0,2:T(4,128)(2,1)}, bf16[3,256,1280]{1,0,2:T(4,128)(2,1)S(1)}) fusion(bf16[6,256,1280]{1,0,2:T(8,128)(2,1)} %get-tuple-element.339, s32[]{:T(128)S(6)} %select_n.52, bf16[6,256,1280]{1,0,2:T(8,128)(2,1)} %get-tuple-element.333), kind=kLoop, calls=%fused_computation.22.clone.1 | loop fusion | bytes 7864324 | tf_op jit(solution)/shard_map/while/body/eval_jaxpr/dynamic_slice | solution.py:85
  385.5 6.4 %concatenate.47 = bf16[768,10,128]{0,2,1:T(8,128)(2,1)} reshape(bf16[3,256,1280]{1,0,2:T(4,128)(2,1)} %get-tuple-element.290) | data formatting | bytes 3932160 | tf_op jit(solution)/shard_map/while/body/eval_jaxpr/concatenate | solution.py:91
  399.6 6.3 %fusion.61 = (f32[10,256]{1,0:T(8,128)S(1)}, f32[10,256,1280]{2,1,0:T(8,128)S(1)}) fusion(pred[1280]{0:T(1024)(128)(4,1)S(1)} %pad_add_fusion.2, bf16[256,10,128]{0,2,1:T(8,128)(2,1)} %bitcast.87, bf16[256,10,128]{2,0,1:T(8,128)(2,1)} %copy.77, bf16[256,10,128]{2,0,1:T(8,128)(2,1)} %copy.78, bf16[768,10,128]{2,0,1:T(8,128)(2,1)} %copy.79), kind=kOutput, calls=%fused_computation.2.clone.1 | convolution fusion | flops 858519040 | bytes 17050880 | tf_op jit(solution)/shard_map/while/body/eval_jaxpr/gia,xia->igx/dot_general | solution.py:24
  410.6 8.8 %divide_convert_fusion.2 = bf16[256,10,128]{0,2,1:T(8,128)(2,1)S(1)} fusion(f32[10,256,1280]{2,1,0:T(8,128)} %copy-done, f32[10,256]{1,0:T(8,128)S(1)} %get-tuple-element.292, pred[1280]{0:T(1024)(128)(4,1)S(1)} %pad_add_fusion.2, bf16[256,10,128]{0,2,1:T(8,128)(2,1)} %bitcast.79, bf16[256,10,128]{0,2,1:T(8,128)(2,1)} %bitcast.80, ...), kind=kOutput, calls=%fused_computation.19.clone.1 | convolution fusion | flops 862453760 | bytes 17061120 | tf_op jit(solution)/shard_map/while/body/eval_jaxpr/wqt,twx->qwx/dot_general | solution.py:31
  430.2 7.4 %constant_dynamic-slice_fusion.10 = (bf16[3,256,1280]{1,0,2:T(4,128)(2,1)}, bf16[3,256,1280]{1,0,2:T(4,128)(2,1)S(1)}) fusion(bf16[6,256,1280]{1,0,2:T(8,128)(2,1)} %get-tuple-element.339, s32[]{:T(128)S(6)} %select_n.52, bf16[6,256,1280]{1,0,2:T(8,128)(2,1)} %get-tuple-element.333), kind=kLoop, calls=%fused_computation.22.clone.1 | loop fusion | bytes 7864324 | tf_op jit(solution)/shard_map/while/body/eval_jaxpr/dynamic_slice | solution.py:85
  437.6 6.4 %concatenate.47 = bf16[768,10,128]{0,2,1:T(8,128)(2,1)} reshape(bf16[3,256,1280]{1,0,2:T(4,128)(2,1)} %get-tuple-element.290) | data formatting | bytes 3932160 | tf_op jit(solution)/shard_map/while/body/eval_jaxpr/concatenate | solution.py:91
  444.0 4.0 copy.79
  451.7 6.3 %fusion.61 = (f32[10,256]{1,0:T(8,128)S(1)}, f32[10,256,1280]{2,1,0:T(8,128)S(1)}) fusion(pred[1280]{0:T(1024)(128)(4,1)S(1)} %pad_add_fusion.2, bf16[256,10,128]{0,2,1:T(8,128)(2,1)} %bitcast.87, bf16[256,10,128]{2,0,1:T(8,128)(2,1)} %copy.77, bf16[256,10,128]{2,0,1:T(8,128)(2,1)} %copy.78, bf16[768,10,128]{2,0,1:T(8,128)(2,1)} %copy.79), kind=kOutput, calls=%fused_computation.2.clone.1 | convolution fusion | flops 858519040 | bytes 17050880 | tf_op jit(solution)/shard_map/while/body/eval_jaxpr/gia,xia->igx/dot_general | solution.py:24
  462.7 8.8 %divide_convert_fusion.2 = bf16[256,10,128]{0,2,1:T(8,128)(2,1)S(1)} fusion(f32[10,256,1280]{2,1,0:T(8,128)} %copy-done, f32[10,256]{1,0:T(8,128)S(1)} %get-tuple-element.292, pred[1280]{0:T(1024)(128)(4,1)S(1)} %pad_add_fusion.2, bf16[256,10,128]{0,2,1:T(8,128)(2,1)} %bitcast.79, bf16[256,10,128]{0,2,1:T(8,128)(2,1)} %bitcast.80, ...), kind=kOutput, calls=%fused_computation.19.clone.1 | convolution fusion | flops 862453760 | bytes 17061120 | tf_op jit(solution)/shard_map/while/body/eval_jaxpr/wqt,twx->qwx/dot_general | solution.py:31
  482.3 7.4 %constant_dynamic-slice_fusion.10 = (bf16[3,256,1280]{1,0,2:T(4,128)(2,1)}, bf16[3,256,1280]{1,0,2:T(4,128)(2,1)S(1)}) fusion(bf16[6,256,1280]{1,0,2:T(8,128)(2,1)} %get-tuple-element.339, s32[]{:T(128)S(6)} %select_n.52, bf16[6,256,1280]{1,0,2:T(8,128)(2,1)} %get-tuple-element.333), kind=kLoop, calls=%fused_computation.22.clone.1 | loop fusion | bytes 7864324 | tf_op jit(solution)/shard_map/while/body/eval_jaxpr/dynamic_slice | solution.py:85
  489.7 6.4 %concatenate.47 = bf16[768,10,128]{0,2,1:T(8,128)(2,1)} reshape(bf16[3,256,1280]{1,0,2:T(4,128)(2,1)} %get-tuple-element.290) | data formatting | bytes 3932160 | tf_op jit(solution)/shard_map/while/body/eval_jaxpr/concatenate | solution.py:91
  503.7 6.3 %fusion.61 = (f32[10,256]{1,0:T(8,128)S(1)}, f32[10,256,1280]{2,1,0:T(8,128)S(1)}) fusion(pred[1280]{0:T(1024)(128)(4,1)S(1)} %pad_add_fusion.2, bf16[256,10,128]{0,2,1:T(8,128)(2,1)} %bitcast.87, bf16[256,10,128]{2,0,1:T(8,128)(2,1)} %copy.77, bf16[256,10,128]{2,0,1:T(8,128)(2,1)} %copy.78, bf16[768,10,128]{2,0,1:T(8,128)(2,1)} %copy.79), kind=kOutput, calls=%fused_computation.2.clone.1 | convolution fusion | flops 858519040 | bytes 17050880 | tf_op jit(solution)/shard_map/while/body/eval_jaxpr/gia,xia->igx/dot_general | solution.py:24
  514.7 8.8 %divide_convert_fusion.2 = bf16[256,10,128]{0,2,1:T(8,128)(2,1)S(1)} fusion(f32[10,256,1280]{2,1,0:T(8,128)} %copy-done, f32[10,256]{1,0:T(8,128)S(1)} %get-tuple-element.292, pred[1280]{0:T(1024)(128)(4,1)S(1)} %pad_add_fusion.2, bf16[256,10,128]{0,2,1:T(8,128)(2,1)} %bitcast.79, bf16[256,10,128]{0,2,1:T(8,128)(2,1)} %bitcast.80, ...), kind=kOutput, calls=%fused_computation.19.clone.1 | convolution fusion | flops 862453760 | bytes 17061120 | tf_op jit(solution)/shard_map/while/body/eval_jaxpr/wqt,twx->qwx/dot_general | solution.py:31
  (119 shorter events, 106.2 us)
Async XLA Ops:
  7.2 143.2 %all-gather.5.cloned.1.call-start = ((), (), s32[]{:S(2)}) async-start(), calls=%async_computation.4 | async-start | bytes 5324800 | tf_op jit(solution)/shard_map/all_gather | solution.py:59
  15.8 266.8 %all-gather.3.cloned.1.call-start = ((), (), s32[]{:S(2)}) async-start(), calls=%async_computation.3 | async-start | bytes 5324800 | tf_op jit(solution)/shard_map/all_gather | solution.py:60
  26.0 14.4 %copy-start.6 = (s32[1,2]{1,0:T(1,128)S(1)}, s32[1,2]{1,0:T(1,128)}, u32[]{:S(2)}) copy-start(s32[1,2]{1,0:T(1,128)} %param.15) | copy-start | bytes 28
  26.0 16.3 %copy-start.3 = (bf16[4,256,1280]{2,1,0:T(8,128)(2,1)S(1)}, bf16[4,256,1280]{2,1,0:T(8,128)(2,1)}, u32[]{:S(2)}) copy-start(bf16[4,256,1280]{2,1,0:T(8,128)(2,1)} %param.10) | copy-start | bytes 7864324
  27.2 33.8 %collective-permute-start.1 = (bf16[256,2560]{1,0:T(8,128)(2,1)}, bf16[256,2560]{1,0:T(8,128)(2,1)}, u32[]{:S(2)}, u32[]{:S(2)}) collective-permute-start(bf16[256,2560]{1,0:T(8,128)(2,1)} %pad_maximum_fusion.3), channel_id=1, source_target_pairs={{4,0},{8,4},{12,8},{16,12},{20,16},{24,20},{28,24},{32,28},{36,32}... | collective-permute-start | bytes 3932168 | tf_op jit(solution)/shard_map/ppermute | solution.py:14
  29.7 39.5 %collective-permute-start = (bf16[256,2560]{1,0:T(8,128)(2,1)}, bf16[256,2560]{1,0:T(8,128)(2,1)}, u32[]{:S(2)}, u32[]{:S(2)}) collective-permute-start(bf16[256,2560]{1,0:T(8,128)(2,1)} %pad_maximum_fusion.2), channel_id=1, source_target_pairs={{0,4},{4,8},{8,12},{12,16},{16,20},{20,24},{24,28},{28,32},{32,36}... | collective-permute-start | bytes 3932168 | tf_op jit(solution)/shard_map/ppermute | solution.py:14
  35.3 14.3 %all-to-all-start.2 = ((bf16[8,4,1280]{2,0,1:T(8,128)(2,1)}), bf16[8,4,1280]{2,0,1:T(8,128)(2,1)S(1)}, u32[]{:S(2)}, u32[]{:S(2)}) async-start(bf16[8,4,1280]{2,0,1:T(8,128)(2,1)} %bitcast.25), calls=%async_computation.2 | async-start | bytes 163840 | tf_op jit(solution)/shard_map/all_to_all | solution.py:48
  77.5 7.7 %copy-start.4 = (bf16[1,256,1280]{1,0,2:T(2,128)(2,1)S(1)}, bf16[1,256,1280]{1,0,2:T(2,128)(2,1)}, u32[]{:S(2)}) copy-start(bf16[1,256,1280]{1,0,2:T(2,128)(2,1)} %copy.42) | copy-start | bytes 1966084
  77.5 7.7 %copy-start.5 = (bf16[1,256,1280]{1,0,2:T(2,128)(2,1)S(1)}, bf16[1,256,1280]{1,0,2:T(2,128)(2,1)}, u32[]{:S(2)}) copy-start(bf16[1,256,1280]{1,0,2:T(2,128)(2,1)} %copy.40) | copy-start | bytes 1966084
  316.4 8.5 %copy-start.1 = (bf16[256,1280]{0,1:T(8,128)(2,1)}, bf16[256,1280]{0,1:T(8,128)(2,1)S(1)}, u32[]{:S(2)}) copy-start(bf16[256,1280]{0,1:T(8,128)(2,1)S(1)} %get-tuple-element.340) | copy-start | bytes 1966084 | tf_op jit(solution)/shard_map/while
  353.8 4.7 copy-start
  358.5 10.0 %copy-start.2 = (bf16[256,1280]{0,1:T(8,128)(2,1)S(1)}, bf16[256,1280]{0,1:T(8,128)(2,1)}, u32[]{:S(2)}) copy-start(bf16[256,1280]{0,1:T(8,128)(2,1)} %copy-done.1) | copy-start | bytes 1966084 | tf_op jit(solution)/shard_map/while
  368.5 8.5 %copy-start.1 = (bf16[256,1280]{0,1:T(8,128)(2,1)}, bf16[256,1280]{0,1:T(8,128)(2,1)S(1)}, u32[]{:S(2)}) copy-start(bf16[256,1280]{0,1:T(8,128)(2,1)S(1)} %get-tuple-element.340) | copy-start | bytes 1966084 | tf_op jit(solution)/shard_map/while
  405.9 4.7 copy-start
  410.6 10.0 %copy-start.2 = (bf16[256,1280]{0,1:T(8,128)(2,1)S(1)}, bf16[256,1280]{0,1:T(8,128)(2,1)}, u32[]{:S(2)}) copy-start(bf16[256,1280]{0,1:T(8,128)(2,1)} %copy-done.1) | copy-start | bytes 1966084 | tf_op jit(solution)/shard_map/while
  420.6 8.5 %copy-start.1 = (bf16[256,1280]{0,1:T(8,128)(2,1)}, bf16[256,1280]{0,1:T(8,128)(2,1)S(1)}, u32[]{:S(2)}) copy-start(bf16[256,1280]{0,1:T(8,128)(2,1)S(1)} %get-tuple-element.340) | copy-start | bytes 1966084 | tf_op jit(solution)/shard_map/while
  458.0 4.7 copy-start
  462.7 10.0 %copy-start.2 = (bf16[256,1280]{0,1:T(8,128)(2,1)S(1)}, bf16[256,1280]{0,1:T(8,128)(2,1)}, u32[]{:S(2)}) copy-start(bf16[256,1280]{0,1:T(8,128)(2,1)} %copy-done.1) | copy-start | bytes 1966084 | tf_op jit(solution)/shard_map/while
  472.6 8.5 %copy-start.1 = (bf16[256,1280]{0,1:T(8,128)(2,1)}, bf16[256,1280]{0,1:T(8,128)(2,1)S(1)}, u32[]{:S(2)}) copy-start(bf16[256,1280]{0,1:T(8,128)(2,1)S(1)} %get-tuple-element.340) | copy-start | bytes 1966084 | tf_op jit(solution)/shard_map/while
  510.0 4.7 copy-start
  514.7 10.0 %copy-start.2 = (bf16[256,1280]{0,1:T(8,128)(2,1)S(1)}, bf16[256,1280]{0,1:T(8,128)(2,1)}, u32[]{:S(2)}) copy-start(bf16[256,1280]{0,1:T(8,128)(2,1)} %copy-done.1) | copy-start | bytes 1966084 | tf_op jit(solution)/shard_map/while
Sparse Core Ops, SparseCore 0:
  16.0 134.3 all-gather.4
  153.9 128.7 all-gather.2
where the time goes:
time: 535 us; the launch traced here: 532 us
  waiting for transfers between devices  203 us (38%)
  local copies, waits for them, and re-layouts  170 us (32%)
  matrix products  68.2 us (13%)
  other arithmetic  27.5 us (5%)
  loops' own time  18.1 us (3%)
  blocking collectives  16.8 us (3%)
  between operations  15.5 us (3%)
  starting transfers between devices  12.1 us (2%)
    all_gather x1, waiting for transfers between devices, local(): lax.all_gather(local_v, 'frames', axis=0, tiled=True)  132 us
    all_gather x1, waiting for transfers between devices, local(): lax.all_gather(local_k, 'frames', axis=0, tiled=True)  59.5 us
    concatenate x16, local copies, waits for them, and re-layouts, one_frame(): keys_set = jnp.concatenate([window_k, picked_k], axis=0)  50.6 us
    dot_general x5, matrix products, attend(): jnp.einsum('wqt,twx->qwx', weights.astype(jnp.bfloat16), value_head_rows,...  39.7 us
    dynamic_slice x4, local copies, waits for them, and re-layouts, one_frame(): lax.dynamic_slice_in_dim(stacked_k, frame_index, 3, 0)  29.6 us
    dot_general x5, matrix products, attend(): jnp.einsum('gia,xia->igx', query_head_rows, key_head_rows, preferred_elem...  28.5 us
    another operation x1, loops' own time, local(): frame_out = lax.map(one_frame, jnp.arange(frame_count, dtype=jnp.int32))  18.1 us
    concatenate x4, local copies, waits for them, and re-layouts, one_frame(): values_set = jnp.concatenate([window_v, picked_v], axis=0)  14.5 us
  transfers between devices with their start and end apart: 5, of which 3 were waited for; matrix products, arithmetic and copies ran while one was open for 8% of the time, Pallas kernels for 0%

commit v1 on v0

v1 whole, which is shorter than its diff:
```python
import math

import jax
import jax.numpy as jnp
from jax import lax
from jax.experimental import pallas as pl
from jax.experimental.pallas import tpu as pltpu
from jax.sharding import PartitionSpec as P

HEAD = 128
XN, ZN, YN = 4, 8, 2
HN = 4
HEADS = 10
CHUNKS = 5
WIDE = 256
PER = WIDE // HEAD
TOK = 256
FEAT = HEADS * HEAD
SCALE = math.log2(math.e) / math.sqrt(HEAD)
F32 = jnp.float32
BF16 = jnp.bfloat16
NT = (((1,), (1,)), ((), ()))
SPANS = ((0, 2), (0, 3), (1, 3), (2, 2))
MESH = pl.DeviceIdType.MESH


def kernel(
    q_hbm, k_hbm, v_hbm, kv_hbm, kq_hbm, nb_hbm,
    out_hbm, kout,
    q, k, v, edge, arr, arrq, ring, send, got, o_st, m_st, l_st, sc, sc_m, out_v,
    qx, ox_s, ox_r, st_s, st_r, nb, nb_s,
    load_sem, out_sem, edge_ss, edge_rs, a_ss, a_rs, aq_ss, aq_rs, nb_ss, nb_rs, loc_sem,
    r_ss, r_rs, s_ss, s_rs, qx_ss, qx_rs, ox_ss, ox_rs, st_ss, st_rs,
):
    f = lax.axis_index("frames")
    hd = lax.axis_index("heads")
    x = f % XN
    z = (f // XN) % ZN
    yh = f // (XN * ZN)
    groups = XN * ZN * YN

    def dev(yh_, z_, x_, h_):
        return ((yh_ * ZN + z_) * XN + x_, h_)

    def remote(src, dst, ss, rs, to):
        return pltpu.make_async_remote_copy(
            src_ref=src, dst_ref=dst, send_sem=ss, recv_sem=rs, device_id=to, device_id_type=MESH
        )

    def loads(ch):
        c = pl.ds(pl.multiple_of(ch * WIDE, WIDE), WIDE)
        return [
            pltpu.make_async_copy(a.at[:, :, c], b.at[:, :, c], load_sem.at[ch, n])
            for n, (a, b) in enumerate(((q_hbm, q), (k_hbm, k), (v_hbm, v)))
        ]

    for ch in range(CHUNKS):
        for cp in loads(ch):
            cp.start()

    nxt = ((f + 1) % groups, hd)
    prv = ((f + groups - 1) % groups, hd)
    mine8 = yh * HN + hd

    def part8(d):
        o = (mine8 + d) % (YN * HN)
        return o // HN, o % HN, o

    zr = dev(yh, (z + 1) % ZN, x, hd)
    zl = dev(yh, (z + ZN - 1) % ZN, x, hd)

    def xpart(j):
        return dev(yh, z, (x + j) % XN, hd)

    barrier = pltpu.get_barrier_semaphore()
    partners = [nxt, prv, zr, zl] + [xpart(j) for j in (1, 2, 3)]
    for d in range(1, 8):
        y8, h8, _ = part8(d)
        partners.append(dev(y8, z, x, h8))
    for p_ in partners:
        pl.semaphore_signal(barrier, inc=1, device_id=p_, device_id_type=MESH)
    pl.semaphore_wait(barrier, len(partners))

    def cols(h_):
        return pl.ds(pl.multiple_of(h_ * FEAT, FEAT), FEAT)

    a_copies, aq_copies = [], []
    for d in range(1, 8):
        y8, h8, o = part8(d)
        a_copies.append(remote(kv_hbm.at[:, cols(h8)], arr.at[mine8], a_ss.at[d], a_rs.at[mine8], dev(y8, z, x, h8)))
    for d in range(1, HN):
        h4 = (hd + d) % HN
        aq_copies.append(remote(kq_hbm.at[:, cols(h4)], arrq.at[hd], aq_ss.at[d], aq_rs.at[hd], dev(yh, z, x, h4)))
    nb_copies = [remote(nb_hbm, nb.at[x], nb_ss.at[j], nb_rs.at[x], xpart(j)) for j in (1, 2, 3)]
    a_own = pltpu.make_async_copy(kv_hbm.at[:, cols(hd)], arr.at[mine8], loc_sem.at[0])
    aq_own = pltpu.make_async_copy(kq_hbm.at[:, cols(hd)], arrq.at[hd], loc_sem.at[1])
    nb_own = pltpu.make_async_copy(nb_hbm, nb.at[x], loc_sem.at[2])
    for cp in a_copies + aq_copies + nb_copies + [a_own, aq_own, nb_own]:
        cp.start()

    edge_copies = [
        remote(k_hbm.at[3], edge.at[0, 0], edge_ss.at[0, 0], edge_rs.at[0, 0], nxt),
        remote(k_hbm.at[0], edge.at[1, 0], edge_ss.at[1, 0], edge_rs.at[1, 0], prv),
        remote(v_hbm.at[3], edge.at[0, 1], edge_ss.at[0, 1], edge_rs.at[0, 1], nxt),
        remote(v_hbm.at[0], edge.at[1, 1], edge_ss.at[1, 1], edge_rs.at[1, 1], prv),
    ]
    for cp in edge_copies:
        cp.start()

    def ring_copies(s):
        a = (z + ZN - s) % ZN
        b = (z + s) % ZN
        src_r = ring.at[a] if s < 3 else ring.at[a, 0]
        src_l = ring.at[b] if s < 3 else ring.at[b, 1]
        return (
            remote(src_r, src_r, r_ss.at[0, s], r_rs.at[0, s], zr),
            remote(src_l, src_l, r_ss.at[1, s], r_rs.at[1, s], zl),
        )

    qx_copies = [remote(qx.at[x], qx.at[x], qx_ss.at[j], qx_rs.at[x], xpart(j)) for j in (1, 2, 3)]

    def service_a():
        a_own.wait()
        aq_own.wait()
        nb_own.wait()
        for d in range(1, 8):
            _, _, o = part8(d)
            remote(arr.at[o], arr.at[o], a_ss.at[d], a_rs.at[o], zr).wait_recv()
        for d in range(1, HN):
            h4 = (hd + d) % HN
            remote(arrq.at[h4], arrq.at[h4], aq_ss.at[d], aq_rs.at[h4], zr).wait_recv()
        for y_ in range(YN):
            for j in range(HN // 2):
                t0 = arr[y_ * HN + 2 * j].astype(F32)
                t1 = arr[y_ * HN + 2 * j + 1].astype(F32)
                r = pl.ds(16 * j, 16)
                ring[z, 0, y_, r] = jnp.concatenate([t0[:8], t1[:8]], 0).astype(BF16)
                ring[z, 1, y_, r] = jnp.concatenate([t0[8:], t1[8:]], 0).astype(BF16)
        for cp in ring_copies(0):
            cp.start()
        for j in range(HN // 2):
            qx[x, pl.ds(16 * j, 16)] = jnp.concatenate([arrq[2 * j], arrq[2 * j + 1]], 0).astype(BF16)
        for cp in qx_copies:
            cp.start()

    def service_ring(s):
        for cp in ring_copies(s - 1):
            cp.wait_recv()
        for cp in ring_copies(s):
            cp.start()

    def cs(h):
        return pl.ds(pl.multiple_of(h * HEAD, HEAD), HEAD)

    def run(units):
        units[0][0](0)
        for j in range(len(units)):
            if j + 1 < len(units):
                units[j + 1][0]((j + 1) % 2)
            units[j][1](j % 2)

    def unit(get_q, get_k, get_v, rows, n, fold, finish, valid=None):
        def scores(slot):
            s = lax.dot_general(get_q(), get_k(), NT, preferred_element_type=F32)
            if valid is not None:
                s = jnp.where(valid, s, -jnp.inf)
            sc[slot, 0:rows, 0:n] = s
            m = jnp.max(s, axis=1, keepdims=True)
            if fold is not None:
                m = jnp.maximum(m, fold[0]())
            sc_m[slot, 0:rows] = m

        def values(slot):
            m = sc_m[slot, 0:rows]
            p = jnp.exp2((sc[slot, 0:rows, 0:n] - m) * SCALE)
            l = jnp.sum(p, axis=1, keepdims=True)
            o = jnp.dot(p.astype(BF16), get_v(), preferred_element_type=F32)
            if fold is not None:
                a = jnp.exp2((fold[0]() - m) * SCALE)
                l = l + fold[1]() * a
                o = o + fold[2]() * a
            finish(m, l, o)

        return scores, values

    def state(h, i):
        return (lambda: m_st[h, i], lambda: l_st[h, i], lambda: o_st[h, i])

    def keep(h, i):
        def finish(m, l, o):
            m_st[h, i] = m
            l_st[h, i] = l
            o_st[h, i] = o

        return finish

    def local_unit(h, i):
        a, n = SPANS[i]
        c = cs(h)
        return unit(
            lambda: q[i, :, c],
            lambda: k[a : a + n, :, c].reshape(n * TOK, HEAD),
            lambda: v[a : a + n, :, c].reshape(n * TOK, HEAD),
            TOK, n * TOK, None, keep(h, i),
        )

    def local_chunk(ch, _):
        for cp in loads(ch):
            cp.wait()
        run([local_unit(ch * PER + j, i) for j in range(PER) for i in range(4)])

        @pl.when(ch == 1)
        def _():
            service_a()

        @pl.when(ch == 3)
        def _():
            service_ring(1)

        return 0

    lax.fori_loop(0, CHUNKS, local_chunk, 0)
    service_ring(2)
    service_ring(3)
    for j in (1, 2, 3):
        xx = (x + j) % XN
        remote(nb.at[xx], nb.at[xx], nb_ss.at[j], nb_rs.at[xx], zr).wait_recv()
        remote(qx.at[xx], qx.at[xx], qx_ss.at[j], qx_rs.at[xx], zr).wait_recv()
    nb_smem = pltpu.make_async_copy(nb, nb_s, loc_sem.at[3])
    nb_smem.start()
    nb_smem.wait()
    for cp in ring_copies(3):
        cp.wait_recv()

    def pick(dst, xx):
        for side in range(2):
            kf = nb_s[xx, side, 0]
            for half in range(2):
                for kind in range(2):
                    blk = ring[2 * (kf % 4) + half, kind, kf // 4]
                    for ch in range(CHUNKS):
                        dst(ch)[side, kind, pl.ds(32 * half, 32)] = blk[:, ch * WIDE : (ch + 1) * WIDE]

    def send_copy(ch, j):
        return remote(send.at[j - 1, ch], got.at[ch, x], s_ss.at[ch, j], s_rs.at[ch, x], xpart(j))

    for j in (1, 3, 2):
        pick(lambda ch: send.at[j - 1, ch], (x + j) % XN)
    for ch in range(CHUNKS):
        for j in (1, 3, 2):
            send_copy(ch, j).start()
    pick(lambda ch: got.at[ch, x], x)

    st_s[...] = jnp.zeros_like(st_s)

    def joint_unit(h):
        c = cs(h)

        def finish(m, l, o):
            ox_s[:, :, c] = (o / l).astype(BF16).reshape(XN, 32, HEAD)
            lane = lax.broadcasted_iota(jnp.int32, (XN * 32, HEAD), 1) == h
            st_s[:, 0] = jnp.where(lane, m, st_s[:, 0].reshape(XN * 32, HEAD)).reshape(XN, 32, HEAD)
            st_s[:, 1] = jnp.where(lane, l, st_s[:, 1].reshape(XN * 32, HEAD)).reshape(XN, 32, HEAD)

        return unit(
            lambda: qx[:, :, c].reshape(XN * 32, HEAD),
            lambda: ring[:, 0, :, :, c].reshape(512, HEAD),
            lambda: ring[:, 1, :, :, c].reshape(512, HEAD),
            XN * 32, 512, None, finish,
        )

    def joint_chunk(ch, _):
        run([joint_unit(ch * PER + j) for j in range(PER)])
        return 0

    lax.fori_loop(0, CHUNKS, joint_chunk, 0)
    ox_copies, st_copies = [], []
    for j in (1, 2, 3):
        xx = (x + j) % XN
        ox_copies.append(remote(ox_s.at[xx], ox_r.at[x], ox_ss.at[j], ox_rs.at[x], xpart(j)))
        st_copies.append(remote(st_s.at[xx], st_r.at[x], st_ss.at[j], st_rs.at[x], xpart(j)))
    for cp in ox_copies + st_copies:
        cp.start()
    ox_r[x] = ox_s[x]
    st_r[x] = st_s[x]

    for cp in edge_copies:
        cp.wait_recv()

    def edge_unit(h, e):
        i = 3 * e
        c = cs(h)
        return unit(
            lambda: q[i, :, c], lambda: edge[e, 0, :, c], lambda: edge[e, 1, :, c],
            TOK, TOK, state(h, i), keep(h, i),
            valid=(f > 0) if e == 0 else (f < groups - 1),
        )

    def edge_chunk(ch, _):
        run([edge_unit(ch * PER + j, e) for j in range(PER) for e in range(2)])
        return 0

    lax.fori_loop(0, CHUNKS, edge_chunk, 0)

    def out_copy(ch):
        c = pl.ds(pl.multiple_of(ch * WIDE, WIDE), WIDE)
        return pltpu.make_async_copy(out_v.at[:, :, c], out_hbm.at[:, :, c], out_sem.at[ch])

    def last_unit(ch, j, i):
        h = ch * PER + j
        c = cs(h)
        w = slice(j * HEAD, (j + 1) * HEAD)

        def finish(m, l, o):
            out_v[i, :, c] = (o / l).astype(BF16)

        return unit(
            lambda: q[i, :, c],
            lambda: got[ch, :, :, 0, :, w].reshape(512, HEAD),
            lambda: got[ch, :, :, 1, :, w].reshape(512, HEAD),
            TOK, 512, state(h, i), finish,
        )

    def last_chunk(ch, _):
        for j in (1, 2, 3):
            xx = (x + j) % XN
            remote(got.at[ch, xx], got.at[ch, xx], s_ss.at[ch, j], s_rs.at[ch, xx], zr).wait_recv()
        run([last_unit(ch, j, i) for j in range(PER) for i in range(4)])
        out_copy(ch).start()
        return 0

    lax.fori_loop(0, CHUNKS, last_chunk, 0)

    for j in (1, 2, 3):
        xx = (x + j) % XN
        remote(ox_r.at[xx], ox_r.at[xx], ox_ss.at[j], ox_rs.at[xx], zr).wait_recv()
        remote(st_r.at[xx], st_r.at[xx], st_ss.at[j], st_rs.at[xx], zr).wait_recv()
    m_all = st_r[:, 0]
    w_all = jnp.exp2((m_all - jnp.max(m_all, axis=0, keepdims=True)) * SCALE) * st_r[:, 1]
    total = jnp.sum(w_all, axis=0, keepdims=True)
    w_all = w_all / jnp.where(total > 0, total, 1.0)
    for h in range(HEADS):
        acc = jnp.zeros((32, HEAD), F32)
        for cl in range(XN):
            acc = acc + ox_r[cl, :, h * HEAD : (h + 1) * HEAD].astype(F32) * w_all[cl, :, h : h + 1]
        kout[:, h * HEAD : (h + 1) * HEAD] = acc.astype(BF16)

    for cp in a_copies + aq_copies + nb_copies + edge_copies + qx_copies + ox_copies + st_copies:
        cp.wait_send()
    for s in range(4):
        for cp in ring_copies(s):
            cp.wait_send()
    for ch in range(CHUNKS):
        for j in (1, 2, 3):
            send_copy(ch, j).wait_send()
        out_copy(ch).wait()


def local(frame_q, frame_k, frame_v, keyframe_q, keyframe_k, keyframe_v, neighbours):
    kv = jnp.concatenate([keyframe_k, keyframe_v], axis=0)
    kq = keyframe_q.astype(F32)
    ids = jnp.pad(jnp.broadcast_to(neighbours.reshape(2, 1), (2, 128)), ((0, 6), (0, 0)))
    dma = pltpu.SemaphoreType.DMA
    any_ = pl.BlockSpec(memory_space=pl.ANY)
    vm = pltpu.VMEM
    frame_out, keyframe_out = pl.pallas_call(
        kernel,
        out_shape=(
            jax.ShapeDtypeStruct(frame_q.shape, BF16),
            jax.ShapeDtypeStruct((32, FEAT), BF16),
        ),
        in_specs=[any_] * 6,
        out_specs=(any_, pl.BlockSpec(memory_space=pltpu.VMEM)),
        scratch_shapes=[
            vm((4, TOK, FEAT), BF16), vm((4, TOK, FEAT), BF16), vm((4, TOK, FEAT), BF16),
            vm((2, 2, TOK, FEAT), BF16),
            vm((YN * HN, 16, FEAT), BF16),
            vm((HN, 8, FEAT), F32),
            vm((ZN, 2, YN, 32, FEAT), BF16),
            vm((3, CHUNKS, 2, 2, 64, WIDE), BF16),
            vm((CHUNKS, XN, 2, 2, 64, WIDE), BF16),
            vm((HEADS, 4, TOK, HEAD), F32),
            vm((HEADS, 4, TOK, 1), F32), vm((HEADS, 4, TOK, 1), F32),
            vm((2, TOK, 3 * TOK), F32), vm((2, TOK, 1), F32),
            vm((4, TOK, FEAT), BF16),
            vm((XN, 32, FEAT), BF16),
            vm((XN, 32, FEAT), BF16), vm((XN, 32, FEAT), BF16),
            vm((XN, 2, 32, HEAD), F32), vm((XN, 2, 32, HEAD), F32),
            vm((XN, 8, 128), jnp.int32), pltpu.SMEM((XN, 8, 128), jnp.int32),
            dma((CHUNKS, 3)), dma((CHUNKS,)), dma((2, 2)), dma((2, 2)),
            dma((8,)), dma((8,)), dma((4,)), dma((4,)), dma((4,)), dma((4,)), dma((4,)),
            dma((2, 4)), dma((2, 4)), dma((CHUNKS, 4)), dma((CHUNKS, 4)),
            dma((4,)), dma((4,)), dma((4,)), dma((4,)), dma((4,)), dma((4,)),
        ],
        compiler_params=pltpu.CompilerParams(
            collective_id=0, has_side_effects=True, vmem_limit_bytes=60 * 2**20
        ),
    )(frame_q, frame_k, frame_v, kv, kq, ids)
    return frame_out, keyframe_out


def solution(mesh):
    placed = (
        P("frames", None, "heads"),
        P("frames", None, "heads"),
        P("frames", None, "heads"),
        P(("frames", "heads"), None),
        P(("frames", "heads"), None),
        P(("frames", "heads"), None),
        P("frames", None),
    )
    return jax.shard_map(
        local,
        mesh=mesh,
        in_specs=placed,
        out_specs=(P("frames", None, "heads"), P("frames", "heads")),
        check_vma=False,
    )
```

time: 535 us -> 123 us (0.23)
  waiting for transfers between devices: 203 us -> 0 us
  local copies, waits for them, and re-layouts: 170 us -> 5.4 us
  Pallas kernels: 0 us -> 113 us
  matrix products: 68.2 us -> 0 us
  other arithmetic: 27.5 us -> 3.16 us
  loops' own time: 18.1 us -> 0 us
  blocking collectives: 16.8 us -> 0 us
  between operations: 15.5 us -> 0.65 us
  starting transfers between devices: 12.1 us -> 0 us
    all_gather x2 -> x0, waiting for transfers between devices: 192 us -> none  [the longest x1 132 us: local(): lax.all_gather(local_v, 'frames', axis=0, tiled=True)]
    pallas_call x0 -> x1, Pallas kernels: none -> 113 us  [local(): pl.pallas_call(kernel, out_shape=(jax.ShapeDtypeStruct(frame_q.shape, BF1...]
    dot_general x10 -> x0, matrix products: 68.2 us -> none  [the longest x5 39.7 us: attend(): jnp.einsum('wqt,twx->qwx', weights.astype(jnp.bfloat16), value_head_rows,...]
    concatenate x20 -> x0, local copies, waits for them, and re-layouts: 65.1 us -> none  [the longest x16 50.6 us: one_frame(): keys_set = jnp.concatenate([window_k, picked_k], axis=0)]
    dynamic_slice x17 -> x0, local copies, waits for them, and re-layouts: 44.2 us -> none  [the longest x4 29.6 us: one_frame(): lax.dynamic_slice_in_dim(stacked_k, frame_index, 3, 0)]
    another operation x1 -> x0, loops' own time: 18.1 us -> none  [local(): frame_out = lax.map(one_frame, jnp.arange(frame_count, dtype=jnp.int32))]
    all_to_all x2 -> x0, blocking collectives: 16.8 us -> none  [the longest x1 8.61 us: local(): lax.all_to_all(keyframe_k, 'heads', split_axis=1, concat_axis=0, tiled=True)]
    broadcast_in_dim x14 -> x0, local copies, waits for them, and re-layouts: 16.6 us -> none  [the longest x2 6.03 us: local(): after[None, :, :feature_width]]
  transfers between devices with their start and end apart: 5 -> 0, of which waited for: 3 -> 0; matrix products, arithmetic and copies ran while one was open for 8% -> 0% of each run, Pallas kernels for 0% -> 0%
where the time goes in v1:
time: 123 us; the launch traced here: 122 us
  Pallas kernels  113 us (92%)
  local copies, waits for them, and re-layouts  5.4 us (4%)
  other arithmetic  3.16 us (3%)
    pallas_call x1, Pallas kernels, local(): pl.pallas_call(kernel, out_shape=(jax.ShapeDtypeStruct(frame_q.shape, BF1...  113 us
    unnamed x4, local copies, waits for them, and re-layouts  4.07 us

profile of v1, /device:TPU:8, one launch (start us, length us, event | category | flops | bytes accessed | tf_op | source)
XLA Modules:
  0.0 121.8 jit_solution(9819720132948317749)
XLA Ops:
  0.6 0.7 pad.6
  1.3 0.7 pad.7.nb_hbm
  2.0 1.6 %convert_element_type.3.kq_hbm = f32[8,5120]{1,0:T(8,128)} convert(bf16[8,5120]{1,0:T(8,128)(2,1)} %param.10) | non-fusion elementwise | flops 40960 | bytes 245760 | tf_op jit(solution)/shard_map/convert_element_type | solution.py:361
  3.5 1.6 %pad_maximum_fusion.kv_hbm = bf16[16,5120]{1,0:T(8,128)(2,1)} fusion(bf16[8,5120]{1,0:T(8,128)(2,1)} %param.12, bf16[8,5120]{1,0:T(8,128)(2,1)} %param.11), kind=kLoop, calls=%fused_computation | loop fusion | flops 327680 | bytes 327680 | tf_op jit(solution)/shard_map/concatenate | solution.py:360
  5.1 112.6 %shard_map.86 = (bf16[4,256,1280]{2,1,0:T(8,128)(2,1)}, bf16[32,1280]{1,0:T(8,128)(2,1)}) custom-call(bf16[4,256,1280]{2,1,0:T(8,128)(2,1)} %q_hbm.1, bf16[4,256,1280]{2,1,0:T(8,128)(2,1)} %k_hbm.1, bf16[4,256,1280]{2,1,0:T(8,128)(2,1)} %v_hbm.1, bf16[16,5120]{1,0:T(8,128)(2,1)} %pad_maximum_fusion.kv_hbm, f32[8,5120]{1,0:T(8,128)} %convert_element_type.3.kq_hbm, ...), custom_call_target="tpu_custom_call" | custom-call | tf_op jit(solution)/shard_map/pallas_call | solution.py:366
  117.7 0.0 copy-start
  117.7 3.4 %copy.11 = bf16[4,256,1280]{2,1,0:T(8,128)(2,1)} copy(bf16[4,256,1280]{2,1,0:T(8,128)(2,1)} %get-tuple-element.4) | data formatting | bytes 5242880
  121.1 0.0 copy-done
  121.1 0.6 copy.12
Async XLA Ops:
  117.7 3.4 %copy-start = (bf16[32,1280]{1,0:T(8,128)(2,1)S(1)}, bf16[32,1280]{1,0:T(8,128)(2,1)}, u32[]{:S(2)}) copy-start(bf16[32,1280]{1,0:T(8,128)(2,1)} %get-tuple-element.5) | copy-start | bytes 245764

commit v2 on v1

v2 whole, which is shorter than its diff:
```python
import math

import jax
import jax.numpy as jnp
from jax import lax
from jax.experimental import pallas as pl
from jax.experimental.pallas import tpu as pltpu
from jax.sharding import PartitionSpec as P

HEAD = 128
XN, ZN, YN = 4, 8, 2
HN = 4
HEADS = 10
CHUNKS = 5
WIDE = 256
PER = WIDE // HEAD
TOK = 256
FEAT = HEADS * HEAD
SCALE = math.log2(math.e) / math.sqrt(HEAD)
F32 = jnp.float32
BF16 = jnp.bfloat16
NT = (((1,), (1,)), ((), ()))
SPANS = ((0, 2), (0, 3), (1, 3), (2, 2))
MESH = pl.DeviceIdType.MESH


def kernel(
    q_hbm, k_hbm, v_hbm, kf_q, kf_k, kf_v, ids,
    out_hbm, kout,
    q, k, v, edge, kv, kq, arr, arrq, ringk, ringv, sndk, sndv, gotk, gotv,
    o_st, m_st, l_st, sc, sc_m, out_v, qx, ox_s, ox_r, st_s, st_r, nb_v, nb, nb_s,
    load_sem, out_sem, edge_ss, edge_rs, fwd_ss, fwd_rs, a_ss, a_rs, aq_ss, aq_rs, nb_ss, nb_rs, loc_sem,
    r_ss, r_rs, sk_ss, sk_rs, sv_ss, sv_rs, qx_ss, qx_rs, ox_ss, ox_rs, st_ss, st_rs,
):
    f = lax.axis_index("frames")
    hd = lax.axis_index("heads")
    x = f % XN
    z = (f // XN) % ZN
    y = f // (XN * ZN)
    xp = x % 2
    groups = XN * ZN * YN

    def dev(y_, z_, x_, h_):
        return ((y_ * ZN + z_) * XN + x_, h_)

    def remote(src, dst, ss, rs, to):
        return pltpu.make_async_remote_copy(
            src_ref=src, dst_ref=dst, send_sem=ss, recv_sem=rs, device_id=to, device_id_type=MESH
        )

    def loads(ch):
        c = pl.ds(pl.multiple_of(ch * WIDE, WIDE), WIDE)
        return [
            pltpu.make_async_copy(a.at[:, :, c], b.at[:, :, c], load_sem.at[ch, n])
            for n, (a, b) in enumerate(((q_hbm, q), (k_hbm, k), (v_hbm, v)))
        ]

    for ch in range(CHUNKS):
        for cp in loads(ch):
            cp.start()

    zr = dev(y, (z + 1) % ZN, x, hd)
    zl = dev(y, (z + ZN - 1) % ZN, x, hd)
    fwd_to = (((f + XN) % groups, hd), ((f + groups - XN) % groups, hd))
    yo = (y + 1) % YN
    right, left = (x + 1) % XN, (x + XN - 1) % XN
    sel = [dev(yo, z, x, hd), dev(y, z, right, hd), dev(y, z, left, hd), dev(yo, z, right, hd), dev(yo, z, left, hd)]
    back = (0, 2, 1, 4, 3)
    barrier = pltpu.get_barrier_semaphore()
    near = []
    me16 = y * HN + hd
    for d in range(1, 16):
        o = (me16 + d) % 8
        near.append(dev(o // HN, z, (x + 2 * (d // 8)) % XN, o % HN))
    partners = near + sel[1:] + [zr, zl] + list(fwd_to)
    for p_ in partners:
        pl.semaphore_signal(barrier, inc=1, device_id=p_, device_id_type=MESH)

    kv[...] = jnp.concatenate([kf_k[...].astype(F32), kf_v[...].astype(F32)], 0).astype(BF16)
    kq[...] = kf_q[...].astype(F32)
    row = lax.broadcasted_iota(jnp.int32, (8, 128), 0)
    nb_v[...] = jnp.where(row == 0, ids[0, 0], ids[0, 1])
    pl.semaphore_wait(barrier, len(partners))

    def cols(h_):
        return pl.ds(pl.multiple_of(h_ * FEAT, FEAT), FEAT)

    ys, hp = hd // 2, hd % 2

    def a_copy(i, xs, h_):
        slot = y * 4 + xs * 2 + hp
        return remote(
            kv.at[:, cols(h_)], arr.at[slot], a_ss.at[i], a_rs.at[slot], dev(ys, z, (x + 2 * xs) % XN, h_)
        )

    a_copies = [a_copy(d, 0, (hd + d) % HN) for d in range(1, HN)] + [a_copy(4 + d, 1, d) for d in range(HN)]
    a_self = a_copy(0, 0, hd)
    own_slot = y * 4 + hp
    a_here = pltpu.make_async_copy(kv.at[:, cols(hd)], arr.at[own_slot], a_rs.at[own_slot])
    stays = ys == y

    for cp in a_copies:
        cp.start()

    @pl.when(stays)
    def _():
        a_here.start()

    @pl.when(jnp.logical_not(stays))
    def _():
        a_self.start()

    aq_copies = [
        remote(kq.at[:, cols((hd + d) % HN)], arrq.at[hd], aq_ss.at[d], aq_rs.at[hd], dev(y, z, x, (hd + d) % HN))
        for d in range(1, HN)
    ]
    nb_copies = [remote(nb_v, nb.at[back[i]], nb_ss.at[i], nb_rs.at[back[i]], sel[i]) for i in range(5)]
    aq_own = pltpu.make_async_copy(kq.at[:, cols(hd)], arrq.at[hd], loc_sem.at[0])
    nb_own = pltpu.make_async_copy(nb_v, nb.at[5], loc_sem.at[1])
    for cp in aq_copies + nb_copies + [aq_own, nb_own]:
        cp.start()

    edge_copies = [
        remote(k_hbm.at[3], edge.at[0, 0], edge_ss.at[0, 0], edge_rs.at[0, 0], sel[1]),
        remote(k_hbm.at[0], edge.at[1, 0], edge_ss.at[1, 0], edge_rs.at[1, 0], sel[2]),
        remote(v_hbm.at[3], edge.at[0, 1], edge_ss.at[0, 1], edge_rs.at[0, 1], sel[1]),
        remote(v_hbm.at[0], edge.at[1, 1], edge_ss.at[1, 1], edge_rs.at[1, 1], sel[2]),
    ]
    for cp in edge_copies:
        cp.start()

    def fwd_copy(e, ch, kind):
        c = pl.ds(pl.multiple_of(ch * WIDE, WIDE), WIDE)
        return remote(
            edge.at[e, kind, :, c], edge.at[2 + e, kind, :, c], fwd_ss.at[ch, kind], fwd_rs.at[ch, kind], fwd_to[e]
        )

    def each_end(fn):
        for e, end in ((0, 0), (1, XN - 1)):
            @pl.when(x == end)
            def _():
                fn(e)

    rings = (ringk, ringv)

    def ring_copies(part, s):
        kind, ysrc = part // 2, part % 2
        r = rings[kind]
        a = (z + ZN - s) % ZN
        b = (z + s) % ZN
        src_r = r.at[a, ysrc] if s < 3 else r.at[a, ysrc, 0:16]
        src_l = r.at[b, ysrc] if s < 3 else r.at[b, ysrc, 16:32]
        return (
            remote(src_r, src_r, r_ss.at[0, part, s], r_rs.at[0, part, s], zr),
            remote(src_l, src_l, r_ss.at[1, part, s], r_rs.at[1, part, s], zl),
        )

    quad = [(a, b) for a, b in ((0, 1), (1, 0), (1, 1))]
    gid = xp * 2 + y

    def quad_dev(a, b):
        return dev((y + b) % 2, z, x - xp + (xp + a) % 2, hd)

    def quad_gid(a, b):
        return ((xp + a) % 2) * 2 + (y + b) % 2

    qx_copies = [
        remote(qx.at[gid], qx.at[gid], qx_ss.at[n], qx_rs.at[gid], quad_dev(a, b)) for n, (a, b) in enumerate(quad)
    ]

    def service_a():
        for slot in range(8):
            remote(arr.at[slot], arr.at[slot], a_ss.at[slot], a_rs.at[slot], zr).wait_recv()
        for ysrc in range(YN):
            for j in range(2):
                t0 = arr[ysrc * 4 + 2 * j].astype(F32)
                t1 = arr[ysrc * 4 + 2 * j + 1].astype(F32)
                r = pl.ds(16 * j, 16)
                ringk[z, ysrc, r] = jnp.concatenate([t0[:8], t1[:8]], 0).astype(BF16)
                ringv[z, ysrc, r] = jnp.concatenate([t0[8:], t1[8:]], 0).astype(BF16)
        for part in (0, 1):
            for cp in ring_copies(part, 0):
                cp.start()

    def service_q():
        aq_own.wait()
        nb_own.wait()
        for d in range(1, HN):
            h4 = (hd + d) % HN
            remote(arrq.at[h4], arrq.at[h4], aq_ss.at[d], aq_rs.at[h4], zr).wait_recv()
        for j in range(HN // 2):
            qx[gid, pl.ds(16 * j, 16)] = jnp.concatenate([arrq[2 * j], arrq[2 * j + 1]], 0).astype(BF16)
        for cp in qx_copies:
            cp.start()

    def service_ring(part, s):
        for cp in ring_copies(part, s - 1):
            cp.wait_recv()
        for cp in ring_copies(part, s):
            cp.start()

    def cs(h):
        return pl.ds(pl.multiple_of(h * HEAD, HEAD), HEAD)

    def run(units):
        units[0][0](0)
        for j in range(len(units)):
            if j + 1 < len(units):
                units[j + 1][0]((j + 1) % 2)
            units[j][1](j % 2)

    def unit(get_q, parts, rows, fold, finish):
        def scores(slot):
            qq = get_q()
            at, top = 0, None
            for get_k, _, n, valid in parts:
                s = lax.dot_general(qq, get_k(), NT, preferred_element_type=F32)
                if valid is not None:
                    s = jnp.where(valid, s, -jnp.inf)
                sc[slot, 0:rows, at : at + n] = s
                for t in range(0, n, HEAD):
                    piece = s[:, t : t + HEAD]
                    top = piece if top is None else jnp.maximum(top, piece)
                at += n
            m = jnp.broadcast_to(jnp.max(top, axis=1, keepdims=True), (rows, HEAD))
            if fold is not None:
                m = jnp.maximum(m, fold[0]())
            sc_m[slot, 0:rows] = m

        def values(slot):
            m = sc_m[slot, 0:rows]
            at, l, o = 0, None, None
            for _, get_v, n, _ in parts:
                ps = []
                for t in range(at, at + n, HEAD):
                    p = jnp.exp2((sc[slot, 0:rows, t : t + HEAD] - m) * SCALE)
                    l = p if l is None else l + p
                    ps.append(p.astype(BF16))
                d = jnp.dot(jnp.concatenate(ps, axis=1), get_v(), preferred_element_type=F32)
                o = d if o is None else o + d
                at += n
            if fold is not None:
                a = jnp.exp2((fold[0]() - m) * SCALE)
                l = l + fold[1]() * a
                o = o + fold[2]() * a
            finish(m, l, o)

        return scores, values

    def local_unit(h, i):
        a, n = SPANS[i]
        c = cs(h)

        def finish(m, l, o):
            m_st[h, i] = m
            l_st[h, i] = l
            o_st[h, i] = o

        return unit(
            lambda: q[i, :, c],
            [(
                lambda: k[a : a + n, :, c].reshape(n * TOK, HEAD),
                lambda: v[a : a + n, :, c].reshape(n * TOK, HEAD),
                n * TOK, None,
            )],
            TOK, None, finish,
        )

    def local_head(h, _):
        @pl.when(h % PER == 0)
        def _():
            for cp in loads(h // PER):
                cp.wait()

        run([local_unit(h, i) for i in range(4)])
        for at, fn in (
            (2, service_a),
            (3, service_q),
            (5, lambda: service_ring(0, 1)),
            (6, lambda: service_ring(1, 1)),
            (8, lambda: service_ring(0, 2)),
            (9, lambda: service_ring(1, 2)),
        ):
            pl.when(h == at)(fn)
        return 0

    lax.fori_loop(0, HEADS, local_head, 0)

    def pick(kind, dst, place, half):
        for side in range(2):
            kf = nb_s[place, side, 0]
            blk = rings[kind][2 * (kf % 4) + half, kf // 4]
            for ch in range(CHUNKS):
                dst[ch, side] = blk[:, ch * WIDE : (ch + 1) * WIDE]

    def pick_all(kind):
        snd, got = ((sndk, gotk), (sndv, gotv))[kind]
        pick(kind, snd.at[0], 0, 0)
        pick(kind, snd.at[1], 0, 1)
        for i in range(1, 5):
            pick(kind, snd.at[1 + i], i, (i + 1) % 2)

    def pick_own(kind):
        got = (gotk, gotv)[kind]
        pick(kind, got.at[0], 5, 0)
        pick(kind, got.at[1], 5, 1)

    def k_copy(i):
        if i == 0:
            return remote(sndk.at[0:2], gotk.at[2:4], sk_ss.at[0], sk_rs.at[0], sel[0])
        return remote(sndk.at[1 + i], gotk.at[3 + i], sk_ss.at[i], sk_rs.at[i], sel[i])

    def v_copy(ch, i):
        if i == 0:
            return remote(sndv.at[0:2, ch], gotv.at[2:4, ch], sv_ss.at[ch, 0], sv_rs.at[ch, 0], sel[0])
        return remote(sndv.at[1 + i, ch], gotv.at[3 + i, ch], sv_ss.at[ch, i], sv_rs.at[ch, i], sel[i])

    service_ring(0, 3)
    service_ring(1, 3)
    for part in (2, 3):
        for cp in ring_copies(part, 0):
            cp.start()
    for i in range(5):
        remote(nb.at[i], nb.at[i], nb_ss.at[i], nb_rs.at[i], zr).wait_recv()
    nb_smem = pltpu.make_async_copy(nb, nb_s, loc_sem.at[2])
    nb_smem.start()
    nb_smem.wait()
    for part in (0, 1):
        for cp in ring_copies(part, 3):
            cp.wait_recv()
    pick_all(0)
    for i in range(5):
        k_copy(i).start()
    for s in (1, 2, 3):
        service_ring(2, s)
        service_ring(3, s)
        if s == 1:
            pick_own(0)
    for part in (2, 3):
        for cp in ring_copies(part, 3):
            cp.wait_recv()
    pick_all(1)
    for ch in range(CHUNKS):
        for i in range(5):
            v_copy(ch, i).start()
    pick_own(1)

    for cp in edge_copies:
        cp.wait_recv()

    def forward(e):
        for ch in range(CHUNKS):
            for kind in range(2):
                fwd_copy(e, ch, kind).start()

    each_end(forward)

    for n, (a, b) in enumerate(quad):
        g = quad_gid(a, b)
        remote(qx.at[g], qx.at[g], qx_ss.at[n], qx_rs.at[g], zr).wait_recv()
    st_s[...] = jnp.zeros_like(st_s)

    def joint_unit(h):
        c = cs(h)

        def finish(m, l, o):
            l = jnp.sum(l, axis=1, keepdims=True)
            ox_s[:, :, c] = (o / l).astype(BF16).reshape(4, 32, HEAD)
            lane = lax.broadcasted_iota(jnp.int32, (128, HEAD), 1) == h
            st_s[:, 0] = jnp.where(lane, m, st_s[:, 0].reshape(128, HEAD)).reshape(4, 32, HEAD)
            st_s[:, 1] = jnp.where(lane, l, st_s[:, 1].reshape(128, HEAD)).reshape(4, 32, HEAD)

        return unit(
            lambda: qx[:, :, c].reshape(128, HEAD),
            [(
                lambda: ringk[:, :, :, c].reshape(512, HEAD),
                lambda: ringv[:, :, :, c].reshape(512, HEAD),
                512, None,
            )],
            128, None, finish,
        )

    def joint_chunk(ch, _):
        run([joint_unit(ch * PER + j) for j in range(PER)])
        return 0

    lax.fori_loop(0, CHUNKS, joint_chunk, 0)
    ox_copies, st_copies = [], []
    for n, (a, b) in enumerate(quad):
        g = quad_gid(a, b)
        ox_copies.append(remote(ox_s.at[g], ox_r.at[gid], ox_ss.at[n], ox_rs.at[gid], quad_dev(a, b)))
        st_copies.append(remote(st_s.at[g], st_r.at[gid], st_ss.at[n], st_rs.at[gid], quad_dev(a, b)))
    for cp in ox_copies + st_copies:
        cp.start()
    ox_r[gid] = ox_s[gid]
    st_r[gid] = st_s[gid]

    def out_copy(ch):
        c = pl.ds(pl.multiple_of(ch * WIDE, WIDE), WIDE)
        return pltpu.make_async_copy(out_v.at[:, :, c], out_hbm.at[:, :, c], out_sem.at[ch])

    before = jnp.where(x == 0, 2, 0)
    after = jnp.where(x == XN - 1, 3, 1)

    def last_unit(ch, j, i):
        h = ch * PER + j
        c = cs(h)
        w = slice(j * HEAD, (j + 1) * HEAD)

        def finish(m, l, o):
            out_v[i, :, c] = (o * (1.0 / jnp.sum(l, axis=1, keepdims=True))).astype(BF16)

        parts = [(
            lambda: gotk[:, ch, :, :, w].reshape(512, HEAD),
            lambda: gotv[:, ch, :, :, w].reshape(512, HEAD),
            512, None,
        )]
        if i == 0:
            parts.append((lambda: edge[before, 0, :, c], lambda: edge[before, 1, :, c], TOK, f > 0))
        if i == 3:
            parts.append((lambda: edge[after, 0, :, c], lambda: edge[after, 1, :, c], TOK, f < groups - 1))
        state = (lambda: m_st[h, i], lambda: l_st[h, i], lambda: o_st[h, i])
        return unit(lambda: q[i, :, c], parts, TOK, state, finish)

    def last_chunk(ch, _):
        for i in range(5):
            v_copy(ch, i).wait_recv()

        def arrived(e):
            for kind in range(2):
                fwd_copy(e, ch, kind).wait_recv()

        each_end(arrived)
        run([last_unit(ch, j, i) for j in range(PER) for i in range(4)])
        out_copy(ch).start()
        return 0

    for i in range(5):
        k_copy(i).wait_recv()
    lax.fori_loop(0, CHUNKS, last_chunk, 0)

    for n, (a, b) in enumerate(quad):
        g = quad_gid(a, b)
        remote(ox_r.at[g], ox_r.at[g], ox_ss.at[n], ox_rs.at[g], zr).wait_recv()
        remote(st_r.at[g], st_r.at[g], st_ss.at[n], st_rs.at[g], zr).wait_recv()
    m_all = st_r[:, 0]
    w_all = jnp.exp2((m_all - jnp.max(m_all, axis=0, keepdims=True)) * SCALE) * st_r[:, 1]
    total = jnp.sum(w_all, axis=0, keepdims=True)
    w_all = w_all / jnp.where(total > 0, total, 1.0)
    for h in range(HEADS):
        acc = jnp.zeros((32, HEAD), F32)
        for cl in range(4):
            acc = acc + ox_r[cl, :, h * HEAD : (h + 1) * HEAD].astype(F32) * w_all[cl, :, h : h + 1]
        kout[:, h * HEAD : (h + 1) * HEAD] = acc.astype(BF16)

    for cp in a_copies + aq_copies + nb_copies + edge_copies + qx_copies + ox_copies + st_copies:
        cp.wait_send()

    @pl.when(jnp.logical_not(stays))
    def _():
        a_self.wait_send()

    def forwarded(e):
        for ch in range(CHUNKS):
            for kind in range(2):
                fwd_copy(e, ch, kind).wait_send()

    each_end(forwarded)
    for part in range(4):
        for s in range(4):
            for cp in ring_copies(part, s):
                cp.wait_send()
    for i in range(5):
        k_copy(i).wait_send()
    for ch in range(CHUNKS):
        for i in range(5):
            v_copy(ch, i).wait_send()
        out_copy(ch).wait()


def local(frame_q, frame_k, frame_v, keyframe_q, keyframe_k, keyframe_v, neighbours):
    dma = pltpu.SemaphoreType.DMA
    any_ = pl.BlockSpec(memory_space=pl.ANY)
    whole = pl.BlockSpec(memory_space=pltpu.VMEM)
    vm = pltpu.VMEM
    frame_out, keyframe_out = pl.pallas_call(
        kernel,
        out_shape=(
            jax.ShapeDtypeStruct(frame_q.shape, BF16),
            jax.ShapeDtypeStruct((32, FEAT), BF16),
        ),
        in_specs=[any_] * 3 + [whole] * 3 + [pl.BlockSpec(memory_space=pltpu.SMEM)],
        out_specs=(any_, whole),
        scratch_shapes=[
            vm((4, TOK, FEAT), BF16), vm((4, TOK, FEAT), BF16), vm((4, TOK, FEAT), BF16),
            vm((4, 2, TOK, FEAT), BF16),
            vm((16, HN * FEAT), BF16), vm((8, HN * FEAT), F32),
            vm((8, 16, FEAT), BF16), vm((HN, 8, FEAT), F32),
            vm((ZN, YN, 32, FEAT), BF16), vm((ZN, YN, 32, FEAT), BF16),
            vm((6, CHUNKS, 2, 32, WIDE), BF16), vm((6, CHUNKS, 2, 32, WIDE), BF16),
            vm((8, CHUNKS, 2, 32, WIDE), BF16), vm((8, CHUNKS, 2, 32, WIDE), BF16),
            vm((HEADS, 4, TOK, HEAD), F32), vm((HEADS, 4, TOK, HEAD), F32), vm((HEADS, 4, TOK, HEAD), F32),
            vm((2, TOK, 3 * TOK), F32), vm((2, TOK, HEAD), F32),
            vm((4, TOK, FEAT), BF16),
            vm((4, 32, FEAT), BF16), vm((4, 32, FEAT), BF16), vm((4, 32, FEAT), BF16),
            vm((4, 2, 32, HEAD), F32), vm((4, 2, 32, HEAD), F32),
            vm((8, 128), jnp.int32), vm((6, 8, 128), jnp.int32), pltpu.SMEM((6, 8, 128), jnp.int32),
            dma((CHUNKS, 3)), dma((CHUNKS,)), dma((2, 2)), dma((2, 2)), dma((CHUNKS, 2)), dma((CHUNKS, 2)),
            dma((8,)), dma((8,)), dma((4,)), dma((4,)), dma((5,)), dma((5,)), dma((3,)),
            dma((2, 4, 4)), dma((2, 4, 4)), dma((5,)), dma((5,)), dma((CHUNKS, 5)), dma((CHUNKS, 5)),
            dma((3,)), dma((4,)), dma((3,)), dma((4,)), dma((3,)), dma((4,)),
        ],
        compiler_params=pltpu.CompilerParams(
            collective_id=0, has_side_effects=True, vmem_limit_bytes=60 * 2**20
        ),
    )(frame_q, frame_k, frame_v, keyframe_q, keyframe_k, keyframe_v, neighbours)
    return frame_out, keyframe_out


def solution(mesh):
    placed = (
        P("frames", None, "heads"),
        P("frames", None, "heads"),
        P("frames", None, "heads"),
        P(("frames", "heads"), None),
        P(("frames", "heads"), None),
        P(("frames", "heads"), None),
        P("frames", None),
    )
    return jax.shard_map(
        local,
        mesh=mesh,
        in_specs=placed,
        out_specs=(P("frames", None, "heads"), P("frames", "heads")),
        check_vma=False,
    )
```

time: 123 us -> 115 us (0.935)
  Pallas kernels: 113 us -> 109 us
  other arithmetic: 3.16 us -> 0 us
  local copies, waits for them, and re-layouts: 5.4 us -> 4.07 us
    pallas_call x1, Pallas kernels: 113 us -> 109 us  [local(): pl.pallas_call(kernel, out_shape=(jax.ShapeDtypeStruct(frame_q.shape, BF1...]
    concatenate x1 -> x0, other arithmetic: 1.6 us -> none  [local(): kv = jnp.concatenate([keyframe_k, keyframe_v], axis=0)]
    convert_element_type x1 -> x0, other arithmetic: 1.56 us -> none  [local(): kq = keyframe_q.astype(F32)]
    pad x2 -> x0, local copies, waits for them, and re-layouts: 1.32 us -> none  [local(): jnp.pad(jnp.broadcast_to(neighbours.reshape(2, 1), (2, 128)), ((0, 6), (0...]
where the time goes in v2:
time: 115 us; the launch traced here: 114 us
  Pallas kernels  109 us (95%)
  local copies, waits for them, and re-layouts  4.07 us (4%)
    pallas_call x1, Pallas kernels, local(): pl.pallas_call(kernel, out_shape=(jax.ShapeDtypeStruct(frame_q.shape, BF1...  109 us
    unnamed x4, local copies, waits for them, and re-layouts  4.07 us

profile of v2, /device:TPU:8, one launch (start us, length us, event | category | flops | bytes accessed | tf_op | source)
XLA Modules:
  0.0 113.7 jit_solution(3914867956506567397)
XLA Ops:
  0.6 109.0 %shard_map.86 = (bf16[4,256,1280]{2,1,0:T(8,128)(2,1)}, bf16[32,1280]{1,0:T(8,128)(2,1)}) custom-call(bf16[4,256,1280]{2,1,0:T(8,128)(2,1)} %q_hbm.1, bf16[4,256,1280]{2,1,0:T(8,128)(2,1)} %k_hbm.1, bf16[4,256,1280]{2,1,0:T(8,128)(2,1)} %v_hbm.1, bf16[8,5120]{1,0:T(8,128)(2,1)} %kf_q.1, bf16[8,5120]{1,0:T(8,128)(2,1)} %kf_k.1, bf16[8,5120]{1,0:T(8,128)(2,1)} %kf_v.1, ...), custom_call_target="tpu_custom_call" | custom-call | tf_op jit(solution)/shard_map/pallas_call | solution.py:486
  109.6 0.0 copy-start
  109.7 3.4 %copy.11 = bf16[4,256,1280]{2,1,0:T(8,128)(2,1)} copy(bf16[4,256,1280]{2,1,0:T(8,128)(2,1)} %get-tuple-element.4) | data formatting | bytes 5242880
  113.1 0.0 copy-done
  113.1 0.6 copy.12
Async XLA Ops:
  109.6 3.4 %copy-start = (bf16[32,1280]{1,0:T(8,128)(2,1)S(1)}, bf16[32,1280]{1,0:T(8,128)(2,1)}, u32[]{:S(2)}) copy-start(bf16[32,1280]{1,0:T(8,128)(2,1)} %get-tuple-element.5) | copy-start | bytes 245764

commit v3 on v2

--- a/solution.py
+++ b/solution.py
@@ -15,6 +15,8 @@
 WIDE = 256
 PER = WIDE // HEAD
 TOK = 256
+HALF = TOK // 2
+SEGS = ((0, 768, (0, 1, 2)), (768, 512, (3, 4)))
 FEAT = HEADS * HEAD
 SCALE = math.log2(math.e) / math.sqrt(HEAD)
 F32 = jnp.float32
@@ -27,9 +29,9 @@
 def kernel(
     q_hbm, k_hbm, v_hbm, kf_q, kf_k, kf_v, ids,
     out_hbm, kout,
-    q, k, v, edge, kv, kq, arr, arrq, ringk, ringv, sndk, sndv, gotk, gotv,
+    q, k, v, edge, kv, kq, arr, arrq, rka, rkb, rva, rvb, rbuf, sndk, sndv, gotk, gotv,
     o_st, m_st, l_st, sc, sc_m, out_v, qx, ox_s, ox_r, st_s, st_r, nb_v, nb, nb_s,
-    load_sem, out_sem, edge_ss, edge_rs, fwd_ss, fwd_rs, a_ss, a_rs, aq_ss, aq_rs, nb_ss, nb_rs, loc_sem,
+    load_sem, out_sem, edge_ss, edge_rs, fwd_ss, fwd_rs, up_ss, up_rs, on_ss, on_rs, a_ss, a_rs, aq_ss, aq_rs, nb_ss, nb_rs, loc_sem,
     r_ss, r_rs, sk_ss, sk_rs, sv_ss, sv_rs, qx_ss, qx_rs, ox_ss, ox_rs, st_ss, st_rs,
 ):
     f = lax.axis_index("frames")
@@ -120,36 +122,61 @@
     for cp in aq_copies + nb_copies + [aq_own, nb_own]:
         cp.start()
 
-    edge_copies = [
-        remote(k_hbm.at[3], edge.at[0, 0], edge_ss.at[0, 0], edge_rs.at[0, 0], sel[1]),
-        remote(k_hbm.at[0], edge.at[1, 0], edge_ss.at[1, 0], edge_rs.at[1, 0], sel[2]),
-        remote(v_hbm.at[3], edge.at[0, 1], edge_ss.at[0, 1], edge_rs.at[0, 1], sel[1]),
-        remote(v_hbm.at[0], edge.at[1, 1], edge_ss.at[1, 1], edge_rs.at[1, 1], sel[2]),
-    ]
-    for cp in edge_copies:
-        cp.start()
+    lo, hi = pl.ds(0, HALF), pl.ds(HALF, HALF)
+    kv_hbm = (k_hbm, v_hbm)
+
+    def edge_copy(e, kind, part):
+        rows = (lo, hi)[part]
+        return remote(
+            kv_hbm[kind].at[3 - 3 * e, rows], edge.at[e, kind, rows],
+            edge_ss.at[e, kind, part], edge_rs.at[e, kind, part], sel[1 + e],
+        )
+
+    first_x, last_x = x == 0, x == XN - 1
+    sends_past = (last_x, first_x)
+    takes_past = (first_x, last_x)
+
+    def when_not(cond, fn):
+        pl.when(jnp.logical_not(cond))(fn)
+
+    for kind in range(2):
+        for e in range(2):
+            edge_copy(e, kind, 0).start()
+            when_not(sends_past[e], lambda: edge_copy(e, kind, 1).start())
+
+    def chunk_cols(ch):
+        return pl.ds(pl.multiple_of(ch * WIDE, WIDE), WIDE)
 
     def fwd_copy(e, ch, kind):
-        c = pl.ds(pl.multiple_of(ch * WIDE, WIDE), WIDE)
+        c = chunk_cols(ch)
         return remote(
-            edge.at[e, kind, :, c], edge.at[2 + e, kind, :, c], fwd_ss.at[ch, kind], fwd_rs.at[ch, kind], fwd_to[e]
-        )
-
-    def each_end(fn):
-        for e, end in ((0, 0), (1, XN - 1)):
-            @pl.when(x == end)
-            def _():
-                fn(e)
-
-    rings = (ringk, ringv)
+            edge.at[e, kind, lo, c], edge.at[2 + e, kind, lo, c], fwd_ss.at[ch, kind], fwd_rs.at[ch, kind], fwd_to[e]
+        )
+
+    def up_copy(e, ch, kind):
+        c = chunk_cols(ch)
+        return remote(
+            kv_hbm[kind].at[3 - 3 * e, hi, c], rbuf.at[kind, :, c], up_ss.at[ch, kind], up_rs.at[ch, kind], fwd_to[e]
+        )
+
+    def on_copy(e, ch, kind):
+        c = chunk_cols(ch)
+        return remote(
+            rbuf.at[kind, :, c], edge.at[2 + e, kind, hi, c], on_ss.at[ch, kind], on_rs.at[ch, kind], sel[1 + e]
+        )
+
+    def each(conds, fn):
+        for e in range(2):
+            pl.when(conds[e])(lambda: fn(e))
+
+    rings = (rka, rkb, rva, rvb)
 
     def ring_copies(part, s):
-        kind, ysrc = part // 2, part % 2
-        r = rings[kind]
+        r = rings[part]
         a = (z + ZN - s) % ZN
         b = (z + s) % ZN
-        src_r = r.at[a, ysrc] if s < 3 else r.at[a, ysrc, 0:16]
-        src_l = r.at[b, ysrc] if s < 3 else r.at[b, ysrc, 16:32]
+        src_r = r.at[a] if s < 3 else r.at[a, :, 0:16]
+        src_l = r.at[b] if s < 3 else r.at[b, :, 16:32]
         return (
             remote(src_r, src_r, r_ss.at[0, part, s], r_rs.at[0, part, s], zr),
             remote(src_l, src_l, r_ss.at[1, part, s], r_rs.at[1, part, s], zl),
@@ -176,11 +203,16 @@
                 t0 = arr[ysrc * 4 + 2 * j].astype(F32)
                 t1 = arr[ysrc * 4 + 2 * j + 1].astype(F32)
                 r = pl.ds(16 * j, 16)
-                ringk[z, ysrc, r] = jnp.concatenate([t0[:8], t1[:8]], 0).astype(BF16)
-                ringv[z, ysrc, r] = jnp.concatenate([t0[8:], t1[8:]], 0).astype(BF16)
-        for part in (0, 1):
-            for cp in ring_copies(part, 0):
-                cp.start()
+                both = (jnp.concatenate([t0[:8], t1[:8]], 0), jnp.concatenate([t0[8:], t1[8:]], 0))
+                for part in range(4):
+                    first, width, _ = SEGS[part % 2]
+                    rings[part][z, ysrc, r] = both[part // 2][:, first : first + width].astype(BF16)
+        begin(0)
+        begin(1)
+
+    def begin(part):
+        for cp in ring_copies(part, 0):
+            cp.start()
 
     def service_q():
         aq_own.wait()
@@ -273,37 +305,43 @@
                 cp.wait()
 
         run([local_unit(h, i) for i in range(4)])
-        for at, fn in (
-            (2, service_a),
-            (3, service_q),
-            (5, lambda: service_ring(0, 1)),
-            (6, lambda: service_ring(1, 1)),
-            (8, lambda: service_ring(0, 2)),
-            (9, lambda: service_ring(1, 2)),
+        for at, fns in (
+            (1, (service_a,)),
+            (2, (service_q,)),
+            (3, (lambda: service_ring(0, 1),)),
+            (4, (lambda: service_ring(1, 1),)),
+            (5, (lambda: service_ring(0, 2),)),
+            (6, (lambda: service_ring(1, 2), lambda: begin(2))),
+            (7, (lambda: service_ring(0, 3),)),
+            (8, (lambda: service_ring(1, 3),)),
+            (9, (lambda: service_ring(2, 1),)),
         ):
-            pl.when(h == at)(fn)
+            @pl.when(h == at)
+            def _():
+                for fn in fns:
+                    fn()
         return 0
 
     lax.fori_loop(0, HEADS, local_head, 0)
 
-    def pick(kind, dst, place, half):
+    def pick(kind, seg, dst, place, half):
         for side in range(2):
             kf = nb_s[place, side, 0]
-            blk = rings[kind][2 * (kf % 4) + half, kf // 4]
-            for ch in range(CHUNKS):
-                dst[ch, side] = blk[:, ch * WIDE : (ch + 1) * WIDE]
-
-    def pick_all(kind):
-        snd, got = ((sndk, gotk), (sndv, gotv))[kind]
-        pick(kind, snd.at[0], 0, 0)
-        pick(kind, snd.at[1], 0, 1)
+            blk = rings[kind * 2 + seg][2 * (kf % 4) + half, kf // 4]
+            for n, ch in enumerate(SEGS[seg][2]):
+                dst[ch, side] = blk[:, n * WIDE : (n + 1) * WIDE]
+
+    def pick_all(kind, seg):
+        snd = (sndk, sndv)[kind]
+        pick(kind, seg, snd.at[0], 0, 0)
+        pick(kind, seg, snd.at[1], 0, 1)
         for i in range(1, 5):
-            pick(kind, snd.at[1 + i], i, (i + 1) % 2)
-
-    def pick_own(kind):
+            pick(kind, seg, snd.at[1 + i], i, (i + 1) % 2)
+
+    def pick_own(kind, seg):
         got = (gotk, gotv)[kind]
-        pick(kind, got.at[0], 5, 0)
-        pick(kind, got.at[1], 5, 1)
+        pick(kind, seg, got.at[0], 5, 0)
+        pick(kind, seg, got.at[1], 5, 1)
 
     def k_copy(i):
         if i == 0:
@@ -315,53 +353,62 @@
             return remote(sndv.at[0:2, ch], gotv.at[2:4, ch], sv_ss.at[ch, 0], sv_rs.at[ch, 0], sel[0])
         return remote(sndv.at[1 + i, ch], gotv.at[3 + i, ch], sv_ss.at[ch, i], sv_rs.at[ch, i], sel[i])
 
-    service_ring(0, 3)
-    service_ring(1, 3)
-    for part in (2, 3):
-        for cp in ring_copies(part, 0):
-            cp.start()
+    def ring_done(part):
+        for cp in ring_copies(part, 3):
+            cp.wait_recv()
+
+    def send_v(seg):
+        pick_all(1, seg)
+        for ch in SEGS[seg][2]:
+            for i in range(5):
+                v_copy(ch, i).start()
+
+    begin(3)
     for i in range(5):
         remote(nb.at[i], nb.at[i], nb_ss.at[i], nb_rs.at[i], zr).wait_recv()
     nb_smem = pltpu.make_async_copy(nb, nb_s, loc_sem.at[2])
     nb_smem.start()
     nb_smem.wait()
-    for part in (0, 1):
-        for cp in ring_copies(part, 3):
-            cp.wait_recv()
-    pick_all(0)
+    ring_done(0)
+    ring_done(1)
+    pick_all(0, 0)
+    pick_all(0, 1)
     for i in range(5):
         k_copy(i).start()
-    for s in (1, 2, 3):
-        service_ring(2, s)
-        service_ring(3, s)
-        if s == 1:
-            pick_own(0)
-    for part in (2, 3):
-        for cp in ring_copies(part, 3):
-            cp.wait_recv()
-    pick_all(1)
-    for ch in range(CHUNKS):
-        for i in range(5):
-            v_copy(ch, i).start()
-    pick_own(1)
-
-    for cp in edge_copies:
-        cp.wait_recv()
-
-    def forward(e):
+    service_ring(2, 2)
+    service_ring(3, 1)
+    pick_own(0, 0)
+    pick_own(0, 1)
+    service_ring(2, 3)
+    service_ring(3, 2)
+    ring_done(2)
+    send_v(0)
+    service_ring(3, 3)
+
+    for kind in range(2):
+        for e in range(2):
+            edge_copy(e, kind, 0).wait_recv()
+
+    def all_chunks(fn):
         for ch in range(CHUNKS):
             for kind in range(2):
-                fwd_copy(e, ch, kind).start()
-
-    each_end(forward)
+                fn(ch, kind)
+
+    each(takes_past, lambda e: all_chunks(lambda ch, kind: fwd_copy(e, ch, kind).start()))
+    each(sends_past, lambda e: all_chunks(lambda ch, kind: up_copy(e, ch, kind).start()))
+    ring_done(3)
+    send_v(1)
+    pick_own(1, 0)
+    pick_own(1, 1)
 
     for n, (a, b) in enumerate(quad):
         g = quad_gid(a, b)
         remote(qx.at[g], qx.at[g], qx_ss.at[n], qx_rs.at[g], zr).wait_recv()
     st_s[...] = jnp.zeros_like(st_s)
 
-    def joint_unit(h):
+    def joint_unit(seg, h):
         c = cs(h)
+        w = cs(h - SEGS[seg][0] // HEAD)
 
         def finish(m, l, o):
             l = jnp.sum(l, axis=1, keepdims=True)
@@ -373,18 +420,21 @@
         return unit(
             lambda: qx[:, :, c].reshape(128, HEAD),
             [(
-                lambda: ringk[:, :, :, c].reshape(512, HEAD),
-                lambda: ringv[:, :, :, c].reshape(512, HEAD),
+                lambda: rings[seg][:, :, :, w].reshape(512, HEAD),
+                lambda: rings[2 + seg][:, :, :, w].reshape(512, HEAD),
                 512, None,
             )],
             128, None, finish,
         )
 
-    def joint_chunk(ch, _):
-        run([joint_unit(ch * PER + j) for j in range(PER)])
-        return 0
-
-    lax.fori_loop(0, CHUNKS, joint_chunk, 0)
+    for seg in range(2):
+        first, width, _ = SEGS[seg]
+
+        def joint_step(n, _):
+            run([joint_unit(seg, first // HEAD + n * PER + j) for j in range(PER)])
+            return 0
+
+        lax.fori_loop(0, width // WIDE, joint_step, 0)
     ox_copies, st_copies = [], []
     for n, (a, b) in enumerate(quad):
         g = quad_gid(a, b)
@@ -426,17 +476,27 @@
         for i in range(5):
             v_copy(ch, i).wait_recv()
 
+        def hand_on(e):
+            for kind in range(2):
+                up_copy(e, ch, kind).wait_recv()
+                on_copy(e, ch, kind).start()
+
         def arrived(e):
             for kind in range(2):
                 fwd_copy(e, ch, kind).wait_recv()
-
-        each_end(arrived)
+                on_copy(e, ch, kind).wait_recv()
+
+        each(sends_past, hand_on)
+        each(takes_past, arrived)
         run([last_unit(ch, j, i) for j in range(PER) for i in range(4)])
         out_copy(ch).start()
         return 0
 
     for i in range(5):
         k_copy(i).wait_recv()
+    for kind in range(2):
+        for e in range(2):
+            when_not(takes_past[e], lambda: edge_copy(e, kind, 1).wait_recv())
     lax.fori_loop(0, CHUNKS, last_chunk, 0)
 
     for n, (a, b) in enumerate(quad):
@@ -453,19 +513,20 @@
             acc = acc + ox_r[cl, :, h * HEAD : (h + 1) * HEAD].astype(F32) * w_all[cl, :, h : h + 1]
         kout[:, h * HEAD : (h + 1) * HEAD] = acc.astype(BF16)
 
-    for cp in a_copies + aq_copies + nb_copies + edge_copies + qx_copies + ox_copies + st_copies:
+    for cp in a_copies + aq_copies + nb_copies + qx_copies + ox_copies + st_copies:
         cp.wait_send()
 
     @pl.when(jnp.logical_not(stays))
     def _():
         a_self.wait_send()
 
-    def forwarded(e):
-        for ch in range(CHUNKS):
-            for kind in range(2):
-                fwd_copy(e, ch, kind).wait_send()
-
-    each_end(forwarded)
+    for kind in range(2):
+        for e in range(2):
+            edge_copy(e, kind, 0).wait_send()
+            when_not(sends_past[e], lambda: edge_copy(e, kind, 1).wait_send())
+    each(takes_past, lambda e: all_chunks(lambda ch, kind: fwd_copy(e, ch, kind).wait_send()))
+    each(sends_past, lambda e: all_chunks(lambda ch, kind: up_copy(e, ch, kind).wait_send()))
+    each(sends_past, lambda e: all_chunks(lambda ch, kind: on_copy(e, ch, kind).wait_send()))
     for part in range(4):
         for s in range(4):
             for cp in ring_copies(part, s):
@@ -496,7 +557,9 @@
             vm((4, 2, TOK, FEAT), BF16),
             vm((16, HN * FEAT), BF16), vm((8, HN * FEAT), F32),
             vm((8, 16, FEAT), BF16), vm((HN, 8, FEAT), F32),
-            vm((ZN, YN, 32, FEAT), BF16), vm((ZN, YN, 32, FEAT), BF16),
+            vm((ZN, YN, 32, SEGS[0][1]), BF16), vm((ZN, YN, 32, SEGS[1][1]), BF16),
+            vm((ZN, YN, 32, SEGS[0][1]), BF16), vm((ZN, YN, 32, SEGS[1][1]), BF16),
+            vm((2, HALF, FEAT), BF16),
             vm((6, CHUNKS, 2, 32, WIDE), BF16), vm((6, CHUNKS, 2, 32, WIDE), BF16),
             vm((8, CHUNKS, 2, 32, WIDE), BF16), vm((8, CHUNKS, 2, 32, WIDE), BF16),
             vm((HEADS, 4, TOK, HEAD), F32), vm((HEADS, 4, TOK, HEAD), F32), vm((HEADS, 4, TOK, HEAD), F32),
@@ -505,7 +568,8 @@
             vm((4, 32, FEAT), BF16), vm((4, 32, FEAT), BF16), vm((4, 32, FEAT), BF16),
             vm((4, 2, 32, HEAD), F32), vm((4, 2, 32, HEAD), F32),
             vm((8, 128), jnp.int32), vm((6, 8, 128), jnp.int32), pltpu.SMEM((6, 8, 128), jnp.int32),
-            dma((CHUNKS, 3)), dma((CHUNKS,)), dma((2, 2)), dma((2, 2)), dma((CHUNKS, 2)), dma((CHUNKS, 2)),
+            dma((CHUNKS, 3)), dma((CHUNKS,)), dma((2, 2, 2)), dma((2, 2, 2)), dma((CHUNKS, 2)), dma((CHUNKS, 2)),
+            dma((CHUNKS, 2)), dma((CHUNKS, 2)), dma((CHUNKS, 2)), dma((CHUNKS, 2)),
             dma((8,)), dma((8,)), dma((4,)), dma((4,)), dma((5,)), dma((5,)), dma((3,)),
             dma((2, 4, 4)), dma((2, 4, 4)), dma((5,)), dma((5,)), dma((CHUNKS, 5)), dma((CHUNKS, 5)),
             dma((3,)), dma((4,)), dma((3,)), dma((4,)), dma((3,)), dma((4,)),

time: 115 us -> 125 us (1.087); the launches traced: 114 us -> 125 us
  Pallas kernels: 109 us -> 120 us
    pallas_call x1, Pallas kernels: 109 us -> 120 us  [local(): pl.pallas_call(kernel, out_shape=(jax.ShapeDtypeStruct(frame_q.shape, BF1...]
where the time goes in v3:
time: 125 us
  Pallas kernels  120 us (96%)
  local copies, waits for them, and re-layouts  4.07 us (3%)
    pallas_call x1, Pallas kernels, local(): pl.pallas_call(kernel, out_shape=(jax.ShapeDtypeStruct(frame_q.shape, BF1...  120 us
    unnamed x4, local copies, waits for them, and re-layouts  4.07 us

profile of v3, /device:TPU:8, one launch (start us, length us, event | category | flops | bytes accessed | tf_op | source)
XLA Modules:
  0.0 125.0 jit_solution(3268324342396089652)
XLA Ops:
  0.6 120.3 %shard_map.86 = (bf16[4,256,1280]{2,1,0:T(8,128)(2,1)}, bf16[32,1280]{1,0:T(8,128)(2,1)}) custom-call(bf16[4,256,1280]{2,1,0:T(8,128)(2,1)} %q_hbm.1, bf16[4,256,1280]{2,1,0:T(8,128)(2,1)} %k_hbm.1, bf16[4,256,1280]{2,1,0:T(8,128)(2,1)} %v_hbm.1, bf16[8,5120]{1,0:T(8,128)(2,1)} %kf_q.1, bf16[8,5120]{1,0:T(8,128)(2,1)} %kf_k.1, bf16[8,5120]{1,0:T(8,128)(2,1)} %kf_v.1, ...), custom_call_target="tpu_custom_call" | custom-call | tf_op jit(solution)/shard_map/pallas_call | solution.py:547
  121.0 0.0 copy-start
  121.0 3.4 %copy.11 = bf16[4,256,1280]{2,1,0:T(8,128)(2,1)} copy(bf16[4,256,1280]{2,1,0:T(8,128)(2,1)} %get-tuple-element.4) | data formatting | bytes 5242880
  124.4 0.0 copy-done
  124.4 0.6 copy.12
Async XLA Ops:
  121.0 3.4 %copy-start = (bf16[32,1280]{1,0:T(8,128)(2,1)S(1)}, bf16[32,1280]{1,0:T(8,128)(2,1)}, u32[]{:S(2)}) copy-start(bf16[32,1280]{1,0:T(8,128)(2,1)} %get-tuple-element.5) | copy-start | bytes 245764

commit v4 on v3

--- a/solution.py
+++ b/solution.py
@@ -16,7 +16,7 @@
 PER = WIDE // HEAD
 TOK = 256
 HALF = TOK // 2
-SEGS = ((0, 768, (0, 1, 2)), (768, 512, (3, 4)))
+SEGS = ((0, 512, (0, 1)), (512, 768, (2, 3, 4)))
 FEAT = HEADS * HEAD
 SCALE = math.log2(math.e) / math.sqrt(HEAD)
 F32 = jnp.float32
@@ -133,8 +133,16 @@
         )
 
     first_x, last_x = x == 0, x == XN - 1
+    inner = groups - XN
     sends_past = (last_x, first_x)
     takes_past = (first_x, last_x)
+    ups = (last_x & (f < inner), first_x & (f >= XN))
+    ons = (last_x & (f >= XN), first_x & (f < inner))
+    fwds = (first_x & (f < inner), last_x & (f >= XN))
+    ends = (first_x & (f >= XN), last_x & (f < inner))
+    cross = (z == ZN - 1, z == 0)
+    early_ups, late_ups = [tuple(u & (c if a else jnp.logical_not(c)) for u, c in zip(ups, cross)) for a in (1, 0)]
+    early_fwds, late_fwds = [tuple(u & (c if a else jnp.logical_not(c)) for u, c in zip(fwds, cross)) for a in (1, 0)]
 
     def when_not(cond, fn):
         pl.when(jnp.logical_not(cond))(fn)
@@ -142,6 +150,8 @@
     for kind in range(2):
         for e in range(2):
             edge_copy(e, kind, 0).start()
+    for kind in range(2):
+        for e in range(2):
             when_not(sends_past[e], lambda: edge_copy(e, kind, 1).start())
 
     def chunk_cols(ch):
@@ -168,6 +178,41 @@
     def each(conds, fn):
         for e in range(2):
             pl.when(conds[e])(lambda: fn(e))
+
+    def both_kinds(fn):
+        for kind in range(2):
+            fn(kind)
+
+    def all_chunks(fn):
+        for ch in range(CHUNKS):
+            for kind in range(2):
+                fn(ch, kind)
+
+    def past_up(ch, where=ups):
+        each(where, lambda e: both_kinds(lambda kind: up_copy(e, ch, kind).start()))
+
+    def past_on(ch):
+        def one(e, kind):
+            up_copy(e, ch, kind).wait_recv()
+            on_copy(e, ch, kind).start()
+
+        each(ons, lambda e: both_kinds(lambda kind: one(e, kind)))
+
+    def past_fwd(ch, where):
+        each(where, lambda e: both_kinds(lambda kind: fwd_copy(e, ch, kind).start()))
+
+    def first_halves():
+        for kind in range(2):
+            for e in range(2):
+                edge_copy(e, kind, 0).wait_recv()
+
+    past_up(0)
+    past_up(1)
+    for e, at in ((0, 0), (1, groups - 1)):
+        @pl.when(f == at)
+        def _():
+            edge[2 + e] = jnp.zeros((2, TOK, FEAT), BF16)
+
 
     rings = (rka, rkb, rva, rvb)
 
@@ -208,7 +253,7 @@
                     first, width, _ = SEGS[part % 2]
                     rings[part][z, ysrc, r] = both[part // 2][:, first : first + width].astype(BF16)
         begin(0)
-        begin(1)
+        begin(2)
 
     def begin(part):
         for cp in ring_copies(part, 0):
@@ -224,6 +269,11 @@
             qx[gid, pl.ds(16 * j, 16)] = jnp.concatenate([arrq[2 * j], arrq[2 * j + 1]], 0).astype(BF16)
         for cp in qx_copies:
             cp.start()
+        for i in range(5):
+            remote(nb.at[i], nb.at[i], nb_ss.at[i], nb_rs.at[i], zr).wait_recv()
+        nb_smem = pltpu.make_async_copy(nb, nb_s, loc_sem.at[2])
+        nb_smem.start()
+        nb_smem.wait()
 
     def service_ring(part, s):
         for cp in ring_copies(part, s - 1):
@@ -309,12 +359,12 @@
             (1, (service_a,)),
             (2, (service_q,)),
             (3, (lambda: service_ring(0, 1),)),
-            (4, (lambda: service_ring(1, 1),)),
+            (4, (lambda: service_ring(2, 1),)),
             (5, (lambda: service_ring(0, 2),)),
-            (6, (lambda: service_ring(1, 2), lambda: begin(2))),
+            (6, (lambda: service_ring(2, 2), lambda: begin(1), lambda: past_up(2, early_ups))),
             (7, (lambda: service_ring(0, 3),)),
-            (8, (lambda: service_ring(1, 3),)),
-            (9, (lambda: service_ring(2, 1),)),
+            (8, (lambda: service_ring(2, 3), lambda: begin(3), lambda: past_on(0), lambda: past_up(3, early_ups))),
+            (9, (lambda: service_ring(1, 1), lambda: past_on(1), lambda: past_up(4, early_ups))),
         ):
             @pl.when(h == at)
             def _():
@@ -343,10 +393,12 @@
         pick(kind, seg, got.at[0], 5, 0)
         pick(kind, seg, got.at[1], 5, 1)
 
-    def k_copy(i):
+    def k_copy(seg, i):
+        chs = SEGS[seg][2]
+        c = slice(chs[0], chs[-1] + 1)
         if i == 0:
-            return remote(sndk.at[0:2], gotk.at[2:4], sk_ss.at[0], sk_rs.at[0], sel[0])
-        return remote(sndk.at[1 + i], gotk.at[3 + i], sk_ss.at[i], sk_rs.at[i], sel[i])
+            return remote(sndk.at[0:2, c], gotk.at[2:4, c], sk_ss.at[seg, 0], sk_rs.at[seg, 0], sel[0])
+        return remote(sndk.at[1 + i, c], gotk.at[3 + i, c], sk_ss.at[seg, i], sk_rs.at[seg, i], sel[i])
 
     def v_copy(ch, i):
         if i == 0:
@@ -357,48 +409,41 @@
         for cp in ring_copies(part, 3):
             cp.wait_recv()
 
+    def send_k(seg):
+        ring_done(seg)
+        pick_all(0, seg)
+        for i in range(5):
+            k_copy(seg, i).start()
+
     def send_v(seg):
+        ring_done(2 + seg)
         pick_all(1, seg)
         for ch in SEGS[seg][2]:
             for i in range(5):
                 v_copy(ch, i).start()
 
-    begin(3)
-    for i in range(5):
-        remote(nb.at[i], nb.at[i], nb_ss.at[i], nb_rs.at[i], zr).wait_recv()
-    nb_smem = pltpu.make_async_copy(nb, nb_s, loc_sem.at[2])
-    nb_smem.start()
-    nb_smem.wait()
-    ring_done(0)
-    ring_done(1)
-    pick_all(0, 0)
-    pick_all(0, 1)
-    for i in range(5):
-        k_copy(i).start()
-    service_ring(2, 2)
+    send_k(0)
     service_ring(3, 1)
+    send_v(0)
+    first_halves()
+    past_fwd(0, early_fwds)
+    service_ring(1, 2)
+    past_fwd(1, early_fwds)
+    service_ring(3, 2)
+    past_fwd(2, early_fwds)
     pick_own(0, 0)
+    service_ring(1, 3)
+    past_fwd(3, early_fwds)
+    service_ring(3, 3)
+    past_fwd(4, early_fwds)
+    for ch in range(CHUNKS):
+        past_fwd(ch, late_fwds)
+        if ch >= 2:
+            past_up(ch, late_ups)
+    pick_own(1, 0)
+    send_k(1)
+    send_v(1)
     pick_own(0, 1)
-    service_ring(2, 3)
-    service_ring(3, 2)
-    ring_done(2)
-    send_v(0)
-    service_ring(3, 3)
-
-    for kind in range(2):
-        for e in range(2):
-            edge_copy(e, kind, 0).wait_recv()
-
-    def all_chunks(fn):
-        for ch in range(CHUNKS):
-            for kind in range(2):
-                fn(ch, kind)
-
-    each(takes_past, lambda e: all_chunks(lambda ch, kind: fwd_copy(e, ch, kind).start()))
-    each(sends_past, lambda e: all_chunks(lambda ch, kind: up_copy(e, ch, kind).start()))
-    ring_done(3)
-    send_v(1)
-    pick_own(1, 0)
     pick_own(1, 1)
 
     for n, (a, b) in enumerate(quad):
@@ -473,27 +518,26 @@
         return unit(lambda: q[i, :, c], parts, TOK, state, finish)
 
     def last_chunk(ch, _):
+        for n in range(3):
+            pl.when(ch == n)(lambda: past_on(n + 2))
         for i in range(5):
             v_copy(ch, i).wait_recv()
-
-        def hand_on(e):
-            for kind in range(2):
-                up_copy(e, ch, kind).wait_recv()
-                on_copy(e, ch, kind).start()
+        for seg in range(2):
+            @pl.when(ch == SEGS[seg][2][0])
+            def _():
+                for i in range(5):
+                    k_copy(seg, i).wait_recv()
 
         def arrived(e):
             for kind in range(2):
                 fwd_copy(e, ch, kind).wait_recv()
                 on_copy(e, ch, kind).wait_recv()
 
-        each(sends_past, hand_on)
-        each(takes_past, arrived)
+        each(ends, arrived)
         run([last_unit(ch, j, i) for j in range(PER) for i in range(4)])
         out_copy(ch).start()
         return 0
 
-    for i in range(5):
-        k_copy(i).wait_recv()
     for kind in range(2):
         for e in range(2):
             when_not(takes_past[e], lambda: edge_copy(e, kind, 1).wait_recv())
@@ -524,15 +568,16 @@
         for e in range(2):
             edge_copy(e, kind, 0).wait_send()
             when_not(sends_past[e], lambda: edge_copy(e, kind, 1).wait_send())
-    each(takes_past, lambda e: all_chunks(lambda ch, kind: fwd_copy(e, ch, kind).wait_send()))
-    each(sends_past, lambda e: all_chunks(lambda ch, kind: up_copy(e, ch, kind).wait_send()))
-    each(sends_past, lambda e: all_chunks(lambda ch, kind: on_copy(e, ch, kind).wait_send()))
+    each(fwds, lambda e: all_chunks(lambda ch, kind: fwd_copy(e, ch, kind).wait_send()))
+    each(ups, lambda e: all_chunks(lambda ch, kind: up_copy(e, ch, kind).wait_send()))
+    each(ons, lambda e: all_chunks(lambda ch, kind: on_copy(e, ch, kind).wait_send()))
     for part in range(4):
         for s in range(4):
             for cp in ring_copies(part, s):
                 cp.wait_send()
-    for i in range(5):
-        k_copy(i).wait_send()
+    for seg in range(2):
+        for i in range(5):
+            k_copy(seg, i).wait_send()
     for ch in range(CHUNKS):
         for i in range(5):
             v_copy(ch, i).wait_send()
@@ -571,7 +616,7 @@
             dma((CHUNKS, 3)), dma((CHUNKS,)), dma((2, 2, 2)), dma((2, 2, 2)), dma((CHUNKS, 2)), dma((CHUNKS, 2)),
             dma((CHUNKS, 2)), dma((CHUNKS, 2)), dma((CHUNKS, 2)), dma((CHUNKS, 2)),
             dma((8,)), dma((8,)), dma((4,)), dma((4,)), dma((5,)), dma((5,)), dma((3,)),
-            dma((2, 4, 4)), dma((2, 4, 4)), dma((5,)), dma((5,)), dma((CHUNKS, 5)), dma((CHUNKS, 5)),
+            dma((2, 4, 4)), dma((2, 4, 4)), dma((2, 5)), dma((2, 5)), dma((CHUNKS, 5)), dma((CHUNKS, 5)),
             dma((3,)), dma((4,)), dma((3,)), dma((4,)), dma((3,)), dma((4,)),
         ],
         compiler_params=pltpu.CompilerParams(

time: 125 us -> 100 us (0.80)
  the two profiles are of different devices: /device:TPU:8 before, /device:TPU:24 now
where the time goes in v4:
time: 100 us
  Pallas kernels  95.4 us (95%)
  local copies, waits for them, and re-layouts  4.07 us (4%)
    pallas_call x1, Pallas kernels, local(): pl.pallas_call(kernel, out_shape=(jax.ShapeDtypeStruct(frame_q.shape, BF1...  95.4 us
    unnamed x4, local copies, waits for them, and re-layouts  4.07 us

profile of v4, /device:TPU:24, one launch (start us, length us, event | category | flops | bytes accessed | tf_op | source)
XLA Modules:
  0.0 100.1 jit_solution(2382318312423482387)
XLA Ops:
  0.6 95.4 %shard_map.86 = (bf16[4,256,1280]{2,1,0:T(8,128)(2,1)}, bf16[32,1280]{1,0:T(8,128)(2,1)}) custom-call(bf16[4,256,1280]{2,1,0:T(8,128)(2,1)} %q_hbm.1, bf16[4,256,1280]{2,1,0:T(8,128)(2,1)} %k_hbm.1, bf16[4,256,1280]{2,1,0:T(8,128)(2,1)} %v_hbm.1, bf16[8,5120]{1,0:T(8,128)(2,1)} %kf_q.1, bf16[8,5120]{1,0:T(8,128)(2,1)} %kf_k.1, bf16[8,5120]{1,0:T(8,128)(2,1)} %kf_v.1, ...), custom_call_target="tpu_custom_call" | custom-call | tf_op jit(solution)/shard_map/pallas_call | solution.py:592
  96.0 0.0 copy-start
  96.0 3.4 %copy.11 = bf16[4,256,1280]{2,1,0:T(8,128)(2,1)} copy(bf16[4,256,1280]{2,1,0:T(8,128)(2,1)} %get-tuple-element.4) | data formatting | bytes 5242880
  99.5 0.0 copy-done
  99.5 0.6 copy.12
Async XLA Ops:
  96.0 3.4 %copy-start = (bf16[32,1280]{1,0:T(8,128)(2,1)S(1)}, bf16[32,1280]{1,0:T(8,128)(2,1)}, u32[]{:S(2)}) copy-start(bf16[32,1280]{1,0:T(8,128)(2,1)} %get-tuple-element.5) | copy-start | bytes 245764

commit v5 on v4

--- a/solution.py
+++ b/solution.py
@@ -29,9 +29,9 @@
 def kernel(
     q_hbm, k_hbm, v_hbm, kf_q, kf_k, kf_v, ids,
     out_hbm, kout,
-    q, k, v, edge, kv, kq, arr, arrq, rka, rkb, rva, rvb, rbuf, sndk, sndv, gotk, gotv,
+    q, k, v, edge, kv, kq, arr, arrq, rka, rkb, rva, rvb, rbuf, yup, yfw, sndk, sndv, gotk, gotv,
     o_st, m_st, l_st, sc, sc_m, out_v, qx, ox_s, ox_r, st_s, st_r, nb_v, nb, nb_s,
-    load_sem, out_sem, edge_ss, edge_rs, fwd_ss, fwd_rs, up_ss, up_rs, on_ss, on_rs, a_ss, a_rs, aq_ss, aq_rs, nb_ss, nb_rs, loc_sem,
+    load_sem, out_sem, edge_ss, edge_rs, fwd_ss, fwd_rs, up_ss, up_rs, on_ss, on_rs, yu_ss, yu_rs, yf_ss, yf_rs, a_ss, a_rs, aq_ss, aq_rs, nb_ss, nb_rs, loc_sem,
     r_ss, r_rs, sk_ss, sk_rs, sv_ss, sv_rs, qx_ss, qx_rs, ox_ss, ox_rs, st_ss, st_rs,
 ):
     f = lax.axis_index("frames")
@@ -63,7 +63,7 @@
 
     zr = dev(y, (z + 1) % ZN, x, hd)
     zl = dev(y, (z + ZN - 1) % ZN, x, hd)
-    fwd_to = (((f + XN) % groups, hd), ((f + groups - XN) % groups, hd))
+    fwd_to = (zr, zl)
     yo = (y + 1) % YN
     right, left = (x + 1) % XN, (x + XN - 1) % XN
     sel = [dev(yo, z, x, hd), dev(y, z, right, hd), dev(y, z, left, hd), dev(yo, z, right, hd), dev(yo, z, left, hd)]
@@ -74,7 +74,7 @@
     for d in range(1, 16):
         o = (me16 + d) % 8
         near.append(dev(o // HN, z, (x + 2 * (d // 8)) % XN, o % HN))
-    partners = near + sel[1:] + [zr, zl] + list(fwd_to)
+    partners = near + sel[1:] + [zr, zl]
     for p_ in partners:
         pl.semaphore_signal(barrier, inc=1, device_id=p_, device_id_type=MESH)
 
@@ -136,13 +136,16 @@
     inner = groups - XN
     sends_past = (last_x, first_x)
     takes_past = (first_x, last_x)
-    ups = (last_x & (f < inner), first_x & (f >= XN))
     ons = (last_x & (f >= XN), first_x & (f < inner))
-    fwds = (first_x & (f < inner), last_x & (f >= XN))
     ends = (first_x & (f >= XN), last_x & (f < inner))
-    cross = (z == ZN - 1, z == 0)
-    early_ups, late_ups = [tuple(u & (c if a else jnp.logical_not(c)) for u, c in zip(ups, cross)) for a in (1, 0)]
-    early_fwds, late_fwds = [tuple(u & (c if a else jnp.logical_not(c)) for u, c in zip(fwds, cross)) for a in (1, 0)]
+    wrap = (z == ZN - 1, z == 0)
+    near_y, far_y = (y == 0, y == YN - 1), (y == YN - 1, y == 0)
+    plain_ups = tuple(u & jnp.logical_not(w) for u, w in zip(sends_past, wrap))
+    cross_ups = tuple(u & w & t for u, w, t in zip(sends_past, wrap, near_y))
+    stand_ups = tuple(u & w & t for u, w, t in zip(sends_past, wrap, far_y))
+    plain_fwds = tuple(u & jnp.logical_not(w) for u, w in zip(takes_past, wrap))
+    cross_fwds = tuple(u & w & t for u, w, t in zip(takes_past, wrap, near_y))
+    stand_fwds = tuple(u & w & t for u, w, t in zip(takes_past, wrap, far_y))
 
     def when_not(cond, fn):
         pl.when(jnp.logical_not(cond))(fn)
@@ -150,23 +153,26 @@
     for kind in range(2):
         for e in range(2):
             edge_copy(e, kind, 0).start()
-    for kind in range(2):
+
+    def second_halves(kind):
         for e in range(2):
             when_not(sends_past[e], lambda: edge_copy(e, kind, 1).start())
 
     def chunk_cols(ch):
         return pl.ds(pl.multiple_of(ch * WIDE, WIDE), WIDE)
 
-    def fwd_copy(e, ch, kind):
+    def fwd_copy(e, ch, kind, stand=False):
         c = chunk_cols(ch)
+        src = yfw.at[kind, :, c] if stand else edge.at[e, kind, lo, c]
         return remote(
-            edge.at[e, kind, lo, c], edge.at[2 + e, kind, lo, c], fwd_ss.at[ch, kind], fwd_rs.at[ch, kind], fwd_to[e]
-        )
-
-    def up_copy(e, ch, kind):
+            src, edge.at[2 + e, kind, lo, c], fwd_ss.at[ch, kind], fwd_rs.at[ch, kind], fwd_to[e]
+        )
+
+    def up_copy(e, ch, kind, stand=False):
         c = chunk_cols(ch)
+        src = yup.at[kind, :, c] if stand else kv_hbm[kind].at[3 - 3 * e, hi, c]
         return remote(
-            kv_hbm[kind].at[3 - 3 * e, hi, c], rbuf.at[kind, :, c], up_ss.at[ch, kind], up_rs.at[ch, kind], fwd_to[e]
+            src, rbuf.at[kind, :, c], up_ss.at[ch, kind], up_rs.at[ch, kind], fwd_to[e]
         )
 
     def on_copy(e, ch, kind):
@@ -188,8 +194,20 @@
             for kind in range(2):
                 fn(ch, kind)
 
-    def past_up(ch, where=ups):
-        each(where, lambda e: both_kinds(lambda kind: up_copy(e, ch, kind).start()))
+    def yup_copy(e, kind):
+        return remote(kv_hbm[kind].at[3 - 3 * e, hi], yup.at[kind], yu_ss.at[kind], yu_rs.at[kind], sel[0])
+
+    def yfw_copy(e, kind):
+        return remote(edge.at[e, kind, lo], yfw.at[kind], yf_ss.at[kind], yf_rs.at[kind], sel[0])
+
+    def past_up(ch, stand=False):
+        where = stand_ups if stand else plain_ups
+        each(where, lambda e: both_kinds(lambda kind: up_copy(e, ch, kind, stand).start()))
+
+    def stand_up_first():
+        each(stand_ups, lambda e: both_kinds(lambda kind: yup_copy(e, kind).wait_recv()))
+        past_up(0, True)
+        past_up(1, True)
 
     def past_on(ch):
         def one(e, kind):
@@ -198,14 +216,19 @@
 
         each(ons, lambda e: both_kinds(lambda kind: one(e, kind)))
 
-    def past_fwd(ch, where):
-        each(where, lambda e: both_kinds(lambda kind: fwd_copy(e, ch, kind).start()))
+    def past_fwd(ch, stand=False):
+        where = stand_fwds if stand else plain_fwds
+        each(where, lambda e: both_kinds(lambda kind: fwd_copy(e, ch, kind, stand).start()))
+
+    def cross_fwd_start():
+        each(cross_fwds, lambda e: both_kinds(lambda kind: yfw_copy(e, kind).start()))
 
     def first_halves():
         for kind in range(2):
             for e in range(2):
                 edge_copy(e, kind, 0).wait_recv()
 
+    each(cross_ups, lambda e: both_kinds(lambda kind: yup_copy(e, kind).start()))
     past_up(0)
     past_up(1)
     for e, at in ((0, 0), (1, groups - 1)):
@@ -357,14 +380,13 @@
         run([local_unit(h, i) for i in range(4)])
         for at, fns in (
             (1, (service_a,)),
-            (2, (service_q,)),
             (3, (lambda: service_ring(0, 1),)),
-            (4, (lambda: service_ring(2, 1),)),
-            (5, (lambda: service_ring(0, 2),)),
-            (6, (lambda: service_ring(2, 2), lambda: begin(1), lambda: past_up(2, early_ups))),
+            (4, (lambda: service_ring(2, 1), lambda: second_halves(0))),
+            (5, (lambda: service_ring(0, 2), first_halves, cross_fwd_start, service_q)),
+            (6, (lambda: service_ring(2, 2), lambda: begin(1), lambda: second_halves(1), stand_up_first)),
             (7, (lambda: service_ring(0, 3),)),
-            (8, (lambda: service_ring(2, 3), lambda: begin(3), lambda: past_on(0), lambda: past_up(3, early_ups))),
-            (9, (lambda: service_ring(1, 1), lambda: past_on(1), lambda: past_up(4, early_ups))),
+            (8, (lambda: service_ring(2, 3), lambda: begin(3), lambda: past_on(0))),
+            (9, (lambda: service_ring(1, 1), lambda: past_on(1))),
         ):
             @pl.when(h == at)
             def _():
@@ -425,24 +447,22 @@
     send_k(0)
     service_ring(3, 1)
     send_v(0)
-    first_halves()
-    past_fwd(0, early_fwds)
     service_ring(1, 2)
-    past_fwd(1, early_fwds)
     service_ring(3, 2)
-    past_fwd(2, early_fwds)
     pick_own(0, 0)
     service_ring(1, 3)
-    past_fwd(3, early_fwds)
     service_ring(3, 3)
-    past_fwd(4, early_fwds)
     for ch in range(CHUNKS):
-        past_fwd(ch, late_fwds)
+        past_fwd(ch)
         if ch >= 2:
-            past_up(ch, late_ups)
+            past_up(ch)
+            past_up(ch, True)
     pick_own(1, 0)
     send_k(1)
     send_v(1)
+    each(stand_fwds, lambda e: both_kinds(lambda kind: yfw_copy(e, kind).wait_recv()))
+    for ch in range(CHUNKS):
+        past_fwd(ch, True)
     pick_own(0, 1)
     pick_own(1, 1)
 
@@ -568,8 +588,12 @@
         for e in range(2):
             edge_copy(e, kind, 0).wait_send()
             when_not(sends_past[e], lambda: edge_copy(e, kind, 1).wait_send())
-    each(fwds, lambda e: all_chunks(lambda ch, kind: fwd_copy(e, ch, kind).wait_send()))
-    each(ups, lambda e: all_chunks(lambda ch, kind: up_copy(e, ch, kind).wait_send()))
+    for group in (plain_fwds, stand_fwds):
+        each(group, lambda e: all_chunks(lambda ch, kind: fwd_copy(e, ch, kind).wait_send()))
+    for group in (plain_ups, stand_ups):
+        each(group, lambda e: all_chunks(lambda ch, kind: up_copy(e, ch, kind).wait_send()))
+    each(cross_ups, lambda e: both_kinds(lambda kind: yup_copy(e, kind).wait_send()))
+    each(cross_fwds, lambda e: both_kinds(lambda kind: yfw_copy(e, kind).wait_send()))
     each(ons, lambda e: all_chunks(lambda ch, kind: on_copy(e, ch, kind).wait_send()))
     for part in range(4):
         for s in range(4):
@@ -604,7 +628,7 @@
             vm((8, 16, FEAT), BF16), vm((HN, 8, FEAT), F32),
             vm((ZN, YN, 32, SEGS[0][1]), BF16), vm((ZN, YN, 32, SEGS[1][1]), BF16),
             vm((ZN, YN, 32, SEGS[0][1]), BF16), vm((ZN, YN, 32, SEGS[1][1]), BF16),
-            vm((2, HALF, FEAT), BF16),
+            vm((2, HALF, FEAT), BF16), vm((2, HALF, FEAT), BF16), vm((2, HALF, FEAT), BF16),
             vm((6, CHUNKS, 2, 32, WIDE), BF16), vm((6, CHUNKS, 2, 32, WIDE), BF16),
             vm((8, CHUNKS, 2, 32, WIDE), BF16), vm((8, CHUNKS, 2, 32, WIDE), BF16),
             vm((HEADS, 4, TOK, HEAD), F32), vm((HEADS, 4, TOK, HEAD), F32), vm((HEADS, 4, TOK, HEAD), F32),
@@ -615,6 +639,7 @@
             vm((8, 128), jnp.int32), vm((6, 8, 128), jnp.int32), pltpu.SMEM((6, 8, 128), jnp.int32),
             dma((CHUNKS, 3)), dma((CHUNKS,)), dma((2, 2, 2)), dma((2, 2, 2)), dma((CHUNKS, 2)), dma((CHUNKS, 2)),
             dma((CHUNKS, 2)), dma((CHUNKS, 2)), dma((CHUNKS, 2)), dma((CHUNKS, 2)),
+            dma((2,)), dma((2,)), dma((2,)), dma((2,)),
             dma((8,)), dma((8,)), dma((4,)), dma((4,)), dma((5,)), dma((5,)), dma((3,)),
             dma((2, 4, 4)), dma((2, 4, 4)), dma((2, 5)), dma((2, 5)), dma((CHUNKS, 5)), dma((CHUNKS, 5)),
             dma((3,)), dma((4,)), dma((3,)), dma((4,)), dma((3,)), dma((4,)),

time: 100 us -> 92.1 us (0.921)
  the two profiles are of different devices: /device:TPU:24 before, /device:TPU:6 now
where the time goes in v5:
time: 92.1 us; the launch traced here: 91.9 us
  Pallas kernels  87.2 us (95%)
  local copies, waits for them, and re-layouts  4.07 us (4%)
    pallas_call x1, Pallas kernels, local(): pl.pallas_call(kernel, out_shape=(jax.ShapeDtypeStruct(frame_q.shape, BF1...  87.2 us
    unnamed x4, local copies, waits for them, and re-layouts  4.07 us

profile of v5, /device:TPU:6, one launch (start us, length us, event | category | flops | bytes accessed | tf_op | source)
XLA Modules:
  0.0 91.9 jit_solution(550920996469409277)
XLA Ops:
  0.6 87.2 %shard_map.86 = (bf16[4,256,1280]{2,1,0:T(8,128)(2,1)}, bf16[32,1280]{1,0:T(8,128)(2,1)}) custom-call(bf16[4,256,1280]{2,1,0:T(8,128)(2,1)} %q_hbm.1, bf16[4,256,1280]{2,1,0:T(8,128)(2,1)} %k_hbm.1, bf16[4,256,1280]{2,1,0:T(8,128)(2,1)} %v_hbm.1, bf16[8,5120]{1,0:T(8,128)(2,1)} %kf_q.1, bf16[8,5120]{1,0:T(8,128)(2,1)} %kf_k.1, bf16[8,5120]{1,0:T(8,128)(2,1)} %kf_v.1, ...), custom_call_target="tpu_custom_call" | custom-call | tf_op jit(solution)/shard_map/pallas_call | solution.py:616
  87.8 0.0 copy-start
  87.9 3.4 %copy.11 = bf16[4,256,1280]{2,1,0:T(8,128)(2,1)} copy(bf16[4,256,1280]{2,1,0:T(8,128)(2,1)} %get-tuple-element.4) | data formatting | bytes 5242880
  91.3 0.0 copy-done
  91.3 0.6 copy.12
Async XLA Ops:
  87.8 3.4 %copy-start = (bf16[32,1280]{1,0:T(8,128)(2,1)S(1)}, bf16[32,1280]{1,0:T(8,128)(2,1)}, u32[]{:S(2)}) copy-start(bf16[32,1280]{1,0:T(8,128)(2,1)} %get-tuple-element.5) | copy-start | bytes 245764
